TPU v7x, 32 devices: a whole 2x2x4 slice. The times are simulated.
32 devices in a mesh: wide: 16 (over z, x, core), narrow: 2 (over y).
Axes of the slice: x: 2, y: 2, z: 4, core: 2. Of those that a mesh axis runs over, the one named last changes fastest.
Arguments:
- tokens: bfloat16 [16384, 768], P(('wide', 'narrow')), may hold values from -6 to 6
- w_qkv: bfloat16 [768, 2304], P('wide'), may hold values from -0.21875 to 0.21875
- w_out: bfloat16 [768, 768], P('wide'), may hold values from -0.625 to 0.625
- w_gate: bfloat16 [768, 3072], P('wide', 'narrow'), may hold values from -0.21875 to 0.21875
- w_value: bfloat16 [768, 3072], P('wide', 'narrow'), may hold values from -0.21875 to 0.21875
- w_down: bfloat16 [3072, 768], P('narrow', 'wide'), may hold values from -0.109375 to 0.109375
- norm_gains: bfloat16 [2, 768], P(None, 'wide'), may hold values from 0.5 to 1.5
- norm_biases: bfloat16 [2, 768], P(None, 'wide'), may hold values from -1.5 to 1.5
- long_count: int32 [16, 2], P('wide', 'narrow'), may hold values from 0 to 1, as said below
- cotangent: bfloat16 [16384, 768], P(('wide', 'narrow')), may hold values from -6 to 6
Outputs:
- layer_output: bfloat16 [16384, 768], P(('wide', 'narrow'))
- input_grad: float32 [16384, 768], P(('wide', 'narrow'))
- grad_qkv: float32 [768, 2304], P('wide')
- grad_out: float32 [768, 768], P('wide')
- grad_gate: float32 [768, 3072], P('wide', 'narrow')
- grad_value: float32 [768, 3072], P('wide', 'narrow')
- grad_down: float32 [3072, 768], P('narrow', 'wide')
- grad_gains: float32 [2, 768], P(None, 'wide')
- grad_biases: float32 [2, 768], P(None, 'wide')
Inputs may be any that keep to these rules, and one draw needn't show every extreme that they name: long_count[w, n] sequences of 512 tokens open the 512 rows of device (w, n); the rest of its rows are sequences of 128 tokens. Every draw has a device with the most and a device with none.
All inputs are finite; a program needn't handle non-finite values.
Results may differ from a plain program's by a relative error of at most 0.02.
Values may be sent and summed in bfloat16 or wider, within the bound.
No kernel may reach another device: no remote copies, remote signals or barrier semaphores. Data moves between devices by JAX's collectives and lax.ppermute only.
A program may use at most 128 MiB of HBM per device.

v0:
```python
import jax
import jax.numpy as jnp
from jax import lax
from jax.sharding import PartitionSpec as P

D = 768
HEADS = 12
HEAD_DIM = 64
LONG = 512
SHORT = 128


def norm_rows(values, gain_row, bias_row):
    center = jnp.mean(values, axis=-1, keepdims=True)
    shifted = values - center
    spread = jnp.mean(shifted * shifted, axis=-1, keepdims=True)
    return shifted * lax.rsqrt(spread + 1e-05) * gain_row + bias_row


def gelu_product(gate_in, value_in):
    return jax.nn.gelu(gate_in, approximate=False) * value_in


def alibi_slopes(heads):
    power = 1 << heads.bit_length() - 1
    first = [2.0 ** (-8.0 * (index + 1) / power) for index in range(power)]
    second = [2.0 ** (-8.0 * (2 * index + 1) / (2 * power)) for index in range(heads - power)]
    return jnp.array(first + second, dtype=jnp.float32)


def alibi_bias(span, heads):
    position = jnp.arange(span)
    distance = jnp.abs(position[:, None] - position[None, :]).astype(jnp.float32)
    slopes = alibi_slopes(heads)
    return slopes[:, None, None] * distance


def block_scores(query_g, key_g, span):
    width = query_g.shape[-1]
    scores = jnp.einsum(
        "bqhd,bkhd->bhqk", query_g, key_g, preferred_element_type=jnp.float32
    ) * width ** (-0.5)
    return scores - alibi_bias(span, query_g.shape[2])


def attend(query_rows, key_rows, value_rows, span):
    rows, heads, width = query_rows.shape
    groups = rows // span
    shape_g = (groups, span, heads, width)
    query_g = query_rows.reshape(shape_g)
    key_g = key_rows.reshape(shape_g)
    value_g = value_rows.reshape(shape_g)
    scores = block_scores(query_g, key_g, span)
    top = jnp.max(scores, axis=-1, keepdims=True)
    expd = jnp.exp(scores - top)
    total = jnp.sum(expd, axis=-1, keepdims=True)
    probs_low = (expd / total).astype(jnp.bfloat16)
    context = jnp.einsum("bhqk,bkhd->bqhd", probs_low, value_g, preferred_element_type=jnp.float32)
    log_total = jnp.transpose((top + jnp.log(total))[..., 0], (0, 2, 1)).reshape(rows, heads)
    return (context.reshape(rows, heads * width), log_total)


def attend_back(query_rows, key_rows, value_rows, log_total, d_context, span):
    rows, heads, width = query_rows.shape
    groups = rows // span
    shape_g = (groups, span, heads, width)
    query_g = query_rows.reshape(shape_g)
    key_g = key_rows.reshape(shape_g)
    value_g = value_rows.reshape(shape_g)
    d_context_g = d_context.reshape(shape_g)
    lse_g = jnp.transpose(log_total.reshape(groups, span, heads), (0, 2, 1))
    scores = block_scores(query_g, key_g, span)
    probs = jnp.exp(scores - lse_g[..., None])
    probs_low = probs.astype(jnp.bfloat16)
    d_probs = jnp.einsum(
        "bqhd,bkhd->bhqk", d_context_g, value_g, preferred_element_type=jnp.float32
    )
    d_values = jnp.einsum(
        "bhqk,bqhd->bkhd", probs_low, d_context_g, preferred_element_type=jnp.float32
    )
    row_dot = jnp.sum(probs * d_probs, axis=-1, keepdims=True)
    d_scores = (probs * (d_probs - row_dot)).astype(jnp.bfloat16)
    scale = width ** (-0.5)
    d_queries = (
        jnp.einsum("bhqk,bkhd->bqhd", d_scores, key_g, preferred_element_type=jnp.float32) * scale
    )
    d_keys = (
        jnp.einsum("bhqk,bqhd->bkhd", d_scores, query_g, preferred_element_type=jnp.float32) * scale
    )
    return jnp.stack([d_queries, d_keys, d_values], axis=2).reshape(rows, 3, heads, width)


def contract_rows(left, right):
    return lax.dot_general(
        left, right, (((0,), (0,)), ((), ())), preferred_element_type=jnp.float32
    )


def contract_cols(left, right):
    return lax.dot_general(
        left, right, (((1,), (1,)), ((), ())), preferred_element_type=jnp.float32
    )


def shards(
    tokens, w_qkv, w_out, w_gate, w_value, w_down, norm_gains, norm_biases, long_count, cotangent
):
    gathered = (
        lax.all_gather(w_qkv, "wide", axis=0, tiled=True),
        lax.all_gather(w_out, "wide", axis=0, tiled=True),
        lax.all_gather(w_gate, "wide", axis=0, tiled=True),
        lax.all_gather(w_value, "wide", axis=0, tiled=True),
        lax.all_gather(w_down, "wide", axis=1, tiled=True),
        lax.all_gather(norm_gains, "wide", axis=1, tiled=True),
        lax.all_gather(norm_biases, "wide", axis=1, tiled=True),
    )
    full_qkv, full_out, wide_gate, wide_value, wide_down, gains_all, biases_all = gathered
    gains_f = gains_all.astype(jnp.float32)
    biases_f = biases_all.astype(jnp.float32)
    rows_dev = tokens.shape[0]
    n_blocks = rows_dev // LONG
    long_here = long_count[0, 0]
    tokens_f = tokens.astype(jnp.float32)
    mixed = jnp.dot(tokens, full_qkv, preferred_element_type=jnp.float32).astype(jnp.bfloat16)
    heads_view = mixed.reshape(n_blocks, LONG, 3, HEADS, HEAD_DIM)
    query_blk = heads_view[:, :, 0]
    key_blk = heads_view[:, :, 1]
    value_blk = heads_view[:, :, 2]
    block_ids = jnp.arange(n_blocks)

    def forward_block(entry):
        block_id, query_rows, key_rows, value_rows = entry
        return lax.cond(
            block_id < long_here,
            lambda operands: attend(operands[0], operands[1], operands[2], LONG),
            lambda operands: attend(operands[0], operands[1], operands[2], SHORT),
            (query_rows, key_rows, value_rows),
        )

    context_f, lse_rows = lax.map(forward_block, (block_ids, query_blk, key_blk, value_blk))
    context = context_f.reshape(rows_dev, D).astype(jnp.bfloat16)
    branch = jnp.dot(context, full_out, preferred_element_type=jnp.float32)
    hidden_in = tokens_f + branch
    normed = norm_rows(hidden_in, gains_f[0], biases_f[0])
    normed_low = normed.astype(jnp.bfloat16)
    all_rows = lax.all_gather(normed_low, "narrow", axis=0, tiled=True)
    gate = jnp.dot(all_rows, wide_gate, preferred_element_type=jnp.float32)
    value_up = jnp.dot(all_rows, wide_value, preferred_element_type=jnp.float32)
    product_f, pull_product = jax.vjp(gelu_product, gate, value_up)
    product = product_f.astype(jnp.bfloat16)
    ffn_out = lax.psum_scatter(
        jnp.dot(product, wide_down, preferred_element_type=jnp.float32),
        "narrow",
        scatter_dimension=0,
        tiled=True,
    )
    out_in = normed + ffn_out
    layer_out, pull_second = jax.vjp(norm_rows, out_in, gains_f[1], biases_f[1])
    d_out, d_gain_two, d_bias_two = pull_second(cotangent.astype(jnp.float32))
    d_ffn = d_out.astype(jnp.bfloat16)
    d_rows = lax.all_gather(d_ffn, "narrow", axis=0, tiled=True)
    grad_down = contract_rows(product, d_rows)
    d_product = contract_cols(d_rows, wide_down)
    d_gate, d_up = pull_product(d_product)
    d_gate_low = d_gate.astype(jnp.bfloat16)
    d_up_low = d_up.astype(jnp.bfloat16)
    grad_gate = contract_rows(all_rows, d_gate_low)
    grad_value = contract_rows(all_rows, d_up_low)
    d_normed = lax.psum_scatter(
        contract_cols(d_gate_low, wide_gate) + contract_cols(d_up_low, wide_value),
        "narrow",
        scatter_dimension=0,
        tiled=True,
    )
    d_normed_total = d_out + d_normed
    unused_out, pull_first = jax.vjp(norm_rows, hidden_in, gains_f[0], biases_f[0])
    d_hidden, d_gain_one, d_bias_one = pull_first(d_normed_total)
    d_branch = d_hidden.astype(jnp.bfloat16)
    grad_out = contract_rows(context, d_branch)
    d_context = contract_cols(d_branch, full_out).astype(jnp.bfloat16)
    d_context_blk = d_context.reshape(n_blocks, LONG, HEADS, HEAD_DIM)

    def backward_block(entry):
        block_id, query_rows, key_rows, value_rows, log_total, d_ctx = entry
        return lax.cond(
            block_id < long_here,
            lambda operands: attend_back(
                operands[0], operands[1], operands[2], operands[3], operands[4], LONG
            ),
            lambda operands: attend_back(
                operands[0], operands[1], operands[2], operands[3], operands[4], SHORT
            ),
            (query_rows, key_rows, value_rows, log_total, d_ctx),
        )

    d_mixed_f = lax.map(
        backward_block, (block_ids, query_blk, key_blk, value_blk, lse_rows, d_context_blk)
    )
    d_mixed = d_mixed_f.reshape(rows_dev, 3 * D).astype(jnp.bfloat16)
    grad_qkv = contract_rows(tokens, d_mixed)
    input_grad = d_hidden + contract_cols(d_mixed, full_qkv)
    grad_gains = jnp.stack([d_gain_one, d_gain_two])
    grad_biases = jnp.stack([d_bias_one, d_bias_two])
    pieces = (
        lax.psum_scatter(
            grad_qkv.astype(jnp.bfloat16), "wide", scatter_dimension=0, tiled=True
        ).astype(jnp.float32),
        lax.psum_scatter(
            grad_out.astype(jnp.bfloat16), "wide", scatter_dimension=0, tiled=True
        ).astype(jnp.float32),
        lax.psum_scatter(
            grad_gate.astype(jnp.bfloat16), "wide", scatter_dimension=0, tiled=True
        ).astype(jnp.float32),
        lax.psum_scatter(
            grad_value.astype(jnp.bfloat16), "wide", scatter_dimension=0, tiled=True
        ).astype(jnp.float32),
        lax.psum_scatter(
            grad_down.astype(jnp.bfloat16), "wide", scatter_dimension=1, tiled=True
        ).astype(jnp.float32),
        lax.psum_scatter(
            grad_gains.astype(jnp.bfloat16), "wide", scatter_dimension=1, tiled=True
        ).astype(jnp.float32),
        lax.psum_scatter(
            grad_biases.astype(jnp.bfloat16), "wide", scatter_dimension=1, tiled=True
        ).astype(jnp.float32),
    )
    qkv_piece, out_piece, gate_piece, value_piece, down_piece, gains_piece, biases_piece = pieces
    qkv_piece, out_piece, gains_piece, biases_piece = (
        lax.psum(qkv_piece.astype(jnp.bfloat16), "narrow").astype(jnp.float32),
        lax.psum(out_piece.astype(jnp.bfloat16), "narrow").astype(jnp.float32),
        lax.psum(gains_piece.astype(jnp.bfloat16), "narrow").astype(jnp.float32),
        lax.psum(biases_piece.astype(jnp.bfloat16), "narrow").astype(jnp.float32),
    )
    return (
        layer_out.astype(jnp.bfloat16),
        input_grad,
        qkv_piece,
        out_piece,
        gate_piece,
        value_piece,
        down_piece,
        gains_piece,
        biases_piece,
    )


def solution(mesh):
    placed = (
        P(("wide", "narrow"), None),
        P("wide", None),
        P("wide", None),
        P("wide", "narrow"),
        P("wide", "narrow"),
        P("narrow", "wide"),
        P(None, "wide"),
        P(None, "wide"),
        P("wide", "narrow"),
        P(("wide", "narrow"), None),
    )
    return jax.shard_map(
        shards,
        mesh=mesh,
        in_specs=placed,
        out_specs=(
            P(("wide", "narrow"), None),
            P(("wide", "narrow"), None),
            P("wide", None),
            P("wide", None),
            P("wide", "narrow"),
            P("wide", "narrow"),
            P("narrow", "wide"),
            P(None, "wide"),
            P(None, "wide"),
        ),
        check_vma=False,
    )
```

profile of v0, /device:TPU:1, one launch (start us, length us, event | category | flops | bytes accessed | tf_op | source)
XLA Modules:
  0.0 892.0 jit_solution(10672600727664725345)
XLA Ops:
  10.1 23.2 %all-gather = bf16[16,48,2]{1,2,0:T(2,128)(2,1)S(1)} all-gather(bf16[1,48,2]{1,2,0:T(2,128)(2,1)} %bitcast.211), channel_id=1, replica_groups=mesh['wide'=16,'narrow'=2] {'wide'}, dimensions={0}, use_global_device_ids=true | all-gather | bytes 3264 | tf_op jit(solution)/shard_map/all_gather | solution.py:114
  33.4 17.6 %all-gather.1 = bf16[16,48,2]{1,2,0:T(2,128)(2,1)S(1)} all-gather(bf16[1,48,2]{1,2,0:T(2,128)(2,1)} %bitcast.212), channel_id=1, replica_groups=mesh['wide'=16,'narrow'=2] {'wide'}, dimensions={0}, use_global_device_ids=true | all-gather | bytes 3264 | tf_op jit(solution)/shard_map/all_gather | solution.py:115
  51.1 8.8 all-gather.10.cloned.1.call-done
  59.9 5.7 convolution_convert_fusion.1
  65.6 4.3 copy.147
  69.9 2.8 slice_bitcast_fusion
  72.7 11.7 %conditional.6 = (f32[512,12]{1,0:T(8,128)S(1)}, bf16[512,768]{0,1:T(8,128)(2,1)S(1)}) conditional(s32[]{:T(128)} %bitcast.35, (bf16[512,12,64]{0,2,1:T(8,128)(2,1)S(1)}, bf16[512,12,64]{0,2,1:T(8,128)(2,1)S(1)}, f32[12]{0:T(128)S(1)}, bf16[512,12,64]{0,2,1:T(8,128)(2,1)}) %tuple.133, (bf16[512,12,64]{0,2,1:T(8,128)(2,1)S(1)}, ...), branch_computations={%region_0.3_spmd, %region_3.6_spmd} | conditional | flops 853665792 | bytes 45334688
  73.1 3.1 fusion.18
  76.2 3.1 fusion.17
  79.3 4.8 fusion.20
  84.3 15.2 %all-gather.12.cloned.1.call-done = bf16[768,768]{1,0:T(8,128)(2,1)} async-done(((bf16[48,768]{1,0:T(8,128)(2,1)}), bf16[768,768]{1,0:T(8,128)(2,1)}) %all-gather.12.cloned.1.call-update) | async-done | bytes 1179664 | tf_op jit(solution)/shard_map/all_gather | solution.py:110
  99.5 2.6 fusion.69
  102.5 1.2 fusion.59
  105.4 37.7 %all-gather.16.cloned.1.call-done = bf16[768,1536]{1,0:T(8,128)(2,1)} async-done(((bf16[48,1536]{1,0:T(8,128)(2,1)}), bf16[768,1536]{1,0:T(8,128)(2,1)}) %all-gather.16.cloned.1.call-update) | async-done | bytes 2359312 | tf_op jit(solution)/shard_map/all_gather | solution.py:111
  143.1 27.6 %all-gather.14.cloned.1.call-done = bf16[1024,768]{1,0:T(8,128)(2,1)} async-done(((bf16[512,768]{1,0:T(8,128)(2,1)}), bf16[1024,768]{1,0:T(8,128)(2,1)}) %all-gather.14.cloned.1.call-update) | async-done | bytes 1572880 | tf_op jit(solution)/shard_map/all_gather | solution.py:146
  170.7 7.4 fusion.71
  178.1 37.5 %all-gather.18.cloned.1.call-done = bf16[768,1536]{1,0:T(8,128)(2,1)} async-done(((bf16[48,1536]{1,0:T(8,128)(2,1)}), bf16[768,1536]{1,0:T(8,128)(2,1)}) %all-gather.18.cloned.1.call-update) | async-done | bytes 2359312 | tf_op jit(solution)/shard_map/all_gather | solution.py:112
  215.6 20.1 %multiply_convert_fusion.3 = (bf16[1024,1536]{1,0:T(8,128)(2,1)}, f32[1024,1536]{1,0:T(8,128)}, f32[1024,1536]{1,0:T(8,128)}) fusion(f32[1024,1536]{1,0:T(8,128)} %fusion.71, bf16[1024,768]{1,0:T(8,128)(2,1)} %all-gather.14.cloned.1.call-done, bf16[768,1536]{1,0:T(8,128)(2,1)} %all-gather.18.cloned.1.call-done), kind=kOutput, calls=%fused_computation.70 | convolution fusion | flops 2519728128 | bytes 25952256 | tf_op jit(solution)/shard_map/dot_general | solution.py:148
  235.7 23.2 %all-gather.20.cloned.1.call-done = bf16[1536,768]{0,1:T(8,128)(2,1)} async-done(((bf16[1536,48]{0,1:T(8,128)(2,1)}), bf16[1536,768]{0,1:T(8,128)(2,1)}) %all-gather.20.cloned.1.call-update) | async-done | bytes 2359312 | tf_op jit(solution)/shard_map/all_gather | solution.py:113
  258.9 7.0 fusion.72
  265.9 41.8 %reduce-scatter.16.cloned.1.call-done = f32[512,768]{1,0:T(8,128)} async-done(((f32[1024,768]{1,0:T(8,128)}), f32[512,768]{1,0:T(8,128)}) %reduce-scatter.16.cloned.1.call-update) | async-done | bytes 1572880 | tf_op jit(solution)/shard_map/reduce_scatter | solution.py:151
  307.7 2.0 fusion.66
  310.8 1.6 fusion.65
  312.4 1.1 copy-done.4
  313.6 1.1 add_convert_fusion.3
  314.9 27.1 %all-gather.22.cloned.1.call-done = bf16[1024,768]{1,0:T(8,128)(2,1)} async-done(((bf16[512,768]{1,0:T(8,128)(2,1)}), bf16[1024,768]{1,0:T(8,128)(2,1)}) %all-gather.22.cloned.1.call-update) | async-done | bytes 1572880 | tf_op jit(solution)/shard_map/all_gather | solution.py:161
  342.0 10.2 %multiply_convert_fusion.2 = (bf16[1024,1536]{1,0:T(8,128)(2,1)S(1)}, bf16[1024,1536]{1,0:T(8,128)(2,1)S(1)}) fusion(f32[1024,1536]{1,0:T(8,128)} %get-tuple-element.276, f32[1024,1536]{1,0:T(8,128)} %fusion.71, f32[1024,1536]{1,0:T(8,128)} %get-tuple-element.293, bf16[1024,768]{1,0:T(8,128)(2,1)} %all-gather.22.cloned.1.call-done, ...), kind=kOutput, calls=%fused_computation.68 | convolution fusion | flops 2444230656 | bytes 29097984 | tf_op jit(solution)/shard_map/dot_general | solution.py:100
  352.2 2.6 fusion.73
  355.7 4.3 convolution_add_fusion
  360.1 6.4 convolution_convert_fusion.2
  366.6 6.9 convolution_convert_fusion.4
  373.6 6.4 convolution_convert_fusion.3
  380.3 23.3 %reduce-scatter.18.cloned.1.call-done = f32[512,768]{1,0:T(8,128)} async-done(((f32[1024,768]{1,0:T(8,128)}), f32[512,768]{1,0:T(8,128)}) %reduce-scatter.18.cloned.1.call-update) | async-done | bytes 1572880 | tf_op jit(solution)/shard_map/reduce_scatter | solution.py:169
  403.5 2.7 multiply_reduce_fusion.2
  406.9 1.1 copy-done.9
  409.2 33.8 %conditional.7 = (bf16[512,2304]{0,1:T(8,128)(2,1)}) conditional(s32[]{:T(128)} %bitcast.35, (bf16[512,12,64]{0,2,1:T(8,128)(2,1)S(1)}, bf16[512,12,64]{0,2,1:T(8,128)(2,1)S(1)}, f32[12]{0:T(128)S(1)}, f32[512,12]{1,0:T(8,128)S(1)}, bf16[512,12,64]{0,2,1:T(8,128)(2,1)S(1)}, /*index=5*/bf16[512,12,64]{0,2,1:T(8,128)(2,1)}) %tuple.135, ...), branch_computations={%region_16.18_spmd, %region_18.20_spmd} | conditional | flops 2049435648 | bytes 115466352
  409.6 7.8 fusion.70
  417.4 1.1 abs_convert_fusion.3
  418.7 7.4 multiply_reduce_fusion.1
  426.1 6.8 multiply_convert_fusion.1
  432.9 2.9 multiply_bitcast_fusion.2
  435.8 2.1 multiply_bitcast_fusion.3
  437.8 2.0 fusion.44
  439.9 3.1 pad_maximum_fusion.1
  443.0 5.7 fusion.53
  448.6 5.8 copy.166
  454.5 1.3 copy-done.10
  456.1 1.9 convolution_convert_fusion.5
  460.3 8.3 reduce-scatter.26.cloned.1.call-done
  468.6 1.6 convert_element_type.191
  470.3 64.7 %reduce-scatter.22.cloned.1.call-done = bf16[48,1536]{1,0:T(8,128)(2,1)} async-done(((bf16[768,1536]{1,0:T(8,128)(2,1)}), bf16[48,1536]{1,0:T(8,128)(2,1)}) %reduce-scatter.22.cloned.1.call-update) | async-done | bytes 147472 | tf_op jit(solution)/shard_map/reduce_scatter | solution.py:211
  534.9 1.6 convert_element_type.187
  536.6 64.1 %reduce-scatter.24.cloned.1.call-done = bf16[48,1536]{1,0:T(8,128)(2,1)} async-done(((bf16[768,1536]{1,0:T(8,128)(2,1)}), bf16[48,1536]{1,0:T(8,128)(2,1)}) %reduce-scatter.24.cloned.1.call-update) | async-done | bytes 147472 | tf_op jit(solution)/shard_map/reduce_scatter | solution.py:214
  600.6 1.6 convert_element_type.189
  602.3 70.1 %reduce-scatter.28.cloned.1.call-done = bf16[48,2304]{1,0:T(8,128)(2,1)} async-done(((bf16[768,2304]{1,0:T(8,128)(2,1)}), bf16[48,2304]{1,0:T(8,128)(2,1)}) %reduce-scatter.28.cloned.1.call-update) | async-done | bytes 221200
  672.4 2.0 copy.167
  674.4 58.9 %reduce-scatter.20.cloned.1.call-done = bf16[48,768]{1,0:T(8,128)(2,1)} async-done(((bf16[768,768]{1,0:T(8,128)(2,1)}), bf16[48,768]{1,0:T(8,128)(2,1)}) %reduce-scatter.20.cloned.1.call-update) | async-done | bytes 73744 | tf_op jit(solution)/shard_map/reduce_scatter | solution.py:208
  733.3 5.9 add_add_fusion.2
  739.2 51.0 %reduce-scatter.30.cloned.1.call-done = bf16[48,2]{1,0:T(8,128)(2,1)} async-done(((bf16[768,2]{1,0:T(8,128)(2,1)}), bf16[48,2]{1,0:T(8,128)(2,1)}) %reduce-scatter.30.cloned.1.call-update) | async-done | bytes 208
  790.9 55.7 %reduce-scatter.32.cloned.1.call-done = bf16[48,2]{1,0:T(8,128)(2,1)} async-done(((bf16[768,2]{1,0:T(8,128)(2,1)}), bf16[48,2]{1,0:T(8,128)(2,1)}) %reduce-scatter.32.cloned.1.call-update) | async-done | bytes 208
  847.4 3.8 all-reduce
  852.3 29.4 %all-reduce.4.cloned.1.call-done = (bf16[48,2304]{0,1:T(8,128)(2,1)}, bf16[48,768]{1,0:T(8,128)(2,1)}) async-done(((bf16[48,2304]{0,1:T(8,128)(2,1)}, bf16[48,768]{1,0:T(8,128)(2,1)}), (bf16[48,2304]{0,1:T(8,128)(2,1)}, bf16[48,768]{1,0:T(8,128)(2,1)})) %all-reduce.4.cloned.1.call-update) | async-done | bytes 294928 | tf_op jit(solution)/shard_map/psum | solution.py:229
  881.7 2.0 copy.156
  883.7 1.6 convert_element_type.185
  (98 shorter events, 14.5 us)
Async XLA Ops:
  7.2 52.7 %all-gather.10.cloned.1.call-start = ((), (), s32[]{:S(2)}) async-start(), calls=%async_computation.9 | async-start | bytes 3760128 | tf_op jit(solution)/shard_map/all_gather | solution.py:109
  7.9 91.6 %all-gather.12.cloned.1.call-start = ((), (), s32[]{:S(2)}) async-start(), calls=%async_computation.10 | async-start | bytes 1253376 | tf_op jit(solution)/shard_map/all_gather | solution.py:110
  8.7 134.5 %all-gather.16.cloned.1.call-start = ((), (), s32[]{:S(2)}) async-start(), calls=%async_computation.12 | async-start | bytes 2506752 | tf_op jit(solution)/shard_map/all_gather | solution.py:111
  9.4 161.3 %all-gather.14.cloned.1.call-start = ((), (), s32[]{:S(2)}) async-start(), calls=%async_computation.11 | async-start | bytes 2359296 | tf_op jit(solution)/shard_map/all_gather | solution.py:146
  69.9 2.8 copy-start.13
  84.3 15.2 %copy-start.11 = (bf16[512,768]{0,1:T(8,128)(2,1)}, bf16[512,768]{0,1:T(8,128)(2,1)S(1)}, u32[]{:S(2)}) copy-start(bf16[512,768]{0,1:T(8,128)(2,1)S(1)} %get-tuple-element.148) | copy-start | bytes 2359300
  103.7 111.9 %all-gather.18.cloned.1.call-start = ((), (), s32[]{:S(2)}) async-start(), calls=%async_computation.13 | async-start | bytes 2506752 | tf_op jit(solution)/shard_map/all_gather | solution.py:112
  104.3 154.6 %all-gather.20.cloned.1.call-start = ((), (), s32[]{:S(2)}) async-start(), calls=%async_computation.14 | async-start | bytes 2506752 | tf_op jit(solution)/shard_map/all_gather | solution.py:113
  104.9 202.9 %reduce-scatter.16.cloned.1.call-start = ((), (), s32[]{:S(2)}) async-start(), calls=%async_computation.15 | async-start | bytes 4718592 | tf_op jit(solution)/shard_map/reduce_scatter | solution.py:151
  265.9 76.2 %all-gather.22.cloned.1.call-start = ((), (), s32[]{:S(2)}) async-start(), calls=%async_computation.16 | async-start | bytes 2359296 | tf_op jit(solution)/shard_map/all_gather | solution.py:161
  307.7 2.3 copy-start.7
  312.4 1.1 copy-start.4
  314.7 88.9 %reduce-scatter.18.cloned.1.call-start = ((), (), s32[]{:S(2)}) async-start(), calls=%async_computation.17 | async-start | bytes 4718592 | tf_op jit(solution)/shard_map/reduce_scatter | solution.py:169
  342.0 10.2 %copy-start.14 = (bf16[768,1536]{1,0:T(8,128)(2,1)S(1)}, bf16[768,1536]{1,0:T(8,128)(2,1)}, u32[]{:S(2)}) copy-start(bf16[768,1536]{1,0:T(8,128)(2,1)} %all-gather.16.cloned.1.call-done) | copy-start | bytes 7077892
  352.2 2.7 copy-start.18
  352.2 3.0 copy-start.17
  352.2 3.4 copy-start.15
  360.0 108.6 %reduce-scatter.26.cloned.1.call-start = ((), (), s32[]{:S(2)}) async-start(), calls=%async_computation.21 | async-start | bytes 2506752 | tf_op jit(solution)/shard_map/reduce_scatter | solution.py:217
  366.6 168.4 %reduce-scatter.22.cloned.1.call-start = ((), (), s32[]{:S(2)}) async-start(), calls=%async_computation.19 | async-start | bytes 2506752 | tf_op jit(solution)/shard_map/reduce_scatter | solution.py:211
  373.5 227.1 %reduce-scatter.24.cloned.1.call-start = ((), (), s32[]{:S(2)}) async-start(), calls=%async_computation.20 | async-start | bytes 2506752 | tf_op jit(solution)/shard_map/reduce_scatter | solution.py:214
  380.0 292.4 %reduce-scatter.28.cloned.1.call-start = ((), (), s32[]{:S(2)}) async-start(), calls=%async_computation.22 | async-start | bytes 3760128
  406.2 1.8 copy-start.16
  406.9 1.1 copy-start.9
  409.6 7.8 copy-start.2
  435.8 2.1 copy-start.3
  454.5 1.4 copy-start.10
  454.5 1.6 copy-start.12
  454.5 3.6 copy-start.8
  454.5 278.7 %reduce-scatter.20.cloned.1.call-start = ((), (), s32[]{:S(2)}) async-start(), calls=%async_computation.18 | async-start | bytes 1253376 | tf_op jit(solution)/shard_map/reduce_scatter | solution.py:208
  458.0 332.2 %reduce-scatter.30.cloned.1.call-start = ((), (), s32[]{:S(2)}) async-start(), calls=%async_computation.23 | async-start | bytes 208896
  459.1 387.5 %reduce-scatter.32.cloned.1.call-start = ((), (), s32[]{:S(2)}) async-start(), calls=%async_computation.24 | async-start | bytes 208896
  460.1 421.6 %all-reduce.4.cloned.1.call-start = ((), (), s32[]{:S(2)}) async-start(), calls=%async_computation.25 | async-start | bytes 1327104 | tf_op jit(solution)/shard_map/psum | solution.py:229
Sparse Core Ops, SparseCore 0:
  10.3 49.5 all-gather.9
  62.1 37.3 all-gather.11
  101.8 41.2 all-gather.15
  145.1 25.5 all-gather.13
  172.8 42.7 all-gather.17
  217.7 41.0 all-gather.19
  266.0 41.7 reduce-scatter.15
  314.8 27.1 all-gather.21
  360.2 43.3 reduce-scatter.17
  407.2 61.4 reduce-scatter.25
  472.9 62.0 reduce-scatter.21
  538.6 62.0 reduce-scatter.23
  605.0 67.3 reduce-scatter.27
  676.8 56.3 reduce-scatter.19
  737.5 52.5 reduce-scatter.29
  793.9 52.6 reduce-scatter.31
  848.9 32.7 all-reduce.3
where the time goes:
time: 900 us; the launch traced here: 892 us
  waiting for transfers between devices  648 us (72%)
  matrix products  124 us (14%)
  blocking collectives  44.5 us (5%)
  other arithmetic  32.7 us (4%)
  local copies, waits for them, and re-layouts  25.6 us (3%)
  between operations  15 us (2%)
    unnamed x20, waiting for transfers between devices  180 us
    reduce_scatter x1, waiting for transfers between devices, shards(): lax.psum_scatter(grad_gate.astype(jnp.bfloat16), 'wide', scatter_dimensio...  64.7 us
    reduce_scatter x1, waiting for transfers between devices, shards(): lax.psum_scatter(grad_value.astype(jnp.bfloat16), 'wide', scatter_dimensi...  64.1 us
    reduce_scatter x1, waiting for transfers between devices, shards(): lax.psum_scatter(grad_out.astype(jnp.bfloat16), 'wide', scatter_dimension...  58.9 us
    reduce_scatter x1, waiting for transfers between devices, shards(): lax.psum_scatter(jnp.dot(product, wide_down, preferred_element_type=jnp.f...  41.8 us
    all_gather x1, waiting for transfers between devices, shards(): lax.all_gather(w_gate, 'wide', axis=0, tiled=True)  37.7 us
    all_gather x1, waiting for transfers between devices, shards(): lax.all_gather(w_value, 'wide', axis=0, tiled=True)  37.5 us
    psum x1, waiting for transfers between devices, shards(): lax.psum(qkv_piece.astype(jnp.bfloat16), 'narrow').astype(jnp.float32)  29.4 us
  transfers between devices with their start and end apart: 17, of which 17 were waited for; matrix products, arithmetic and copies ran while one was open for 16% of the time, Pallas kernels for 0%

commit v1 on v0

--- a/solution.py
+++ b/solution.py
@@ -1,6 +1,11 @@
+import functools
+
 import jax
 import jax.numpy as jnp
+import numpy as np
 from jax import lax
+from jax.experimental import pallas as pl
+from jax.experimental.pallas import tpu as pltpu
 from jax.sharding import PartitionSpec as P
 
 D = 768
@@ -102,7 +107,7 @@
     )
 
 
-def shards(
+def general_shards(
     tokens, w_qkv, w_out, w_gate, w_value, w_down, norm_gains, norm_biases, long_count, cotangent
 ):
     gathered = (
@@ -244,7 +249,850 @@
     )
 
 
+AXES = ("wide", "narrow")
+F32 = jnp.float32
+BF16 = jnp.bfloat16
+VMEM_LIMIT = 56 * 1024 * 1024
+PAIR = 2 * HEAD_DIM
+
+
+def dot(left, right):
+    return jnp.dot(left, right, preferred_element_type=F32)
+
+
+class Plane:
+    def __init__(self, wide, narrow):
+        self.size = {"z": wide // 4, "a": 2, "b": 2, "core": 2, "y": narrow}
+        self.pairs = {}
+        count = wide * narrow
+        for dim, size in self.size.items():
+            for step in range(1, size):
+                self.pairs[dim, step] = [(i, self.partner(i, dim, step)) for i in range(count)]
+        w = lax.axis_index("wide")
+        self.z, self.x, self.core = w // 4, (w // 2) % 2, w % 2
+        self.y = lax.axis_index("narrow")
+
+    @staticmethod
+    def partner(i, dim, step):
+        z, x, c, y = i // 8, (i // 4) % 2, (i // 2) % 2, i % 2
+        if dim == "z":
+            z ^= step
+        elif dim == "core":
+            c ^= 1
+        elif dim == "y" or (dim == "a") == (c == 1):
+            y ^= 1
+        else:
+            x ^= 1
+        return ((z * 2 + x) * 2 + c) * 2 + y
+
+    def swap(self, value, dim, step=1):
+        return lax.ppermute(value, AXES, self.pairs[dim, step])
+
+    def gather(self, value, order):
+        held = value[None]
+        for place, dim in enumerate(order):
+            parts = [held] + [self.swap(held, dim, k) for k in range(1, self.size[dim])]
+            if place == len(order) - 1:
+                return parts
+            held = jnp.concatenate(parts, axis=0)
+
+    def reduce(self, blocks, order):
+        for dim in reversed(order):
+            size = self.size[dim]
+            blocks = blocks.reshape((size, -1) + blocks.shape[1:])
+            got = [self.swap(blocks[k], dim, k) for k in range(1, size)]
+            total = blocks[0].astype(F32)
+            for part in got:
+                total = total + part.astype(F32)
+            blocks = total.astype(BF16)
+        return total[0]
+
+    def tables(self, order, numbered):
+        sizes = [self.size[dim] for dim in order]
+        number = np.arange(int(np.prod(sizes)))
+        rest, digit = number, {}
+        for dim, size in zip(order, sizes):
+            digit[dim] = rest % size
+            rest = rest // size
+        first = self.core == 0
+        a_here = jnp.where(first, self.x, self.y)
+        b_here = jnp.where(first, self.y, self.x)
+        z = digit["z"] ^ self.z
+        a = digit["a"] ^ a_here
+        b = digit["b"] ^ b_here
+        x, y = jnp.where(first, a, b), jnp.where(first, b, a)
+        forward = numbered(z, x, y).astype(jnp.int32)
+        places = {(zz, xx, yy): int(numbered(zz, xx, yy)) for zz in range(self.size["z"]) for xx in range(2) for yy in range(2)}
+        by_place = sorted(places, key=places.get)
+        pz, px, py = (np.array(v) for v in zip(*by_place))
+        rel = {"z": pz ^ self.z, "a": jnp.where(first, px, py) ^ a_here, "b": jnp.where(first, py, px) ^ b_here}
+        back, scale = 0, 1
+        for dim, size in zip(order, sizes):
+            back = back + rel[dim] * scale
+            scale *= size
+        return forward, back.astype(jnp.int32)
+
+
+def smem():
+    return pl.BlockSpec(memory_space=pltpu.SMEM)
+
+
+def whole(shape):
+    zeros = (0,) * len(shape)
+    return pl.BlockSpec(tuple(shape), lambda *_: zeros)
+
+
+def kernel_call(body, grid, ins, outs, scratch=(), flops=0, name=None):
+    size = sum(a.size * a.dtype.itemsize for a, _ in ins)
+    size += sum(int(np.prod(s)) * np.dtype(d).itemsize for s, d, _ in outs)
+    return pl.pallas_call(
+        body,
+        grid=grid,
+        in_specs=[spec for _, spec in ins],
+        out_specs=[spec for _, _, spec in outs],
+        out_shape=[jax.ShapeDtypeStruct(s, d) for s, d, _ in outs],
+        scratch_shapes=list(scratch),
+        compiler_params=pltpu.CompilerParams(
+            dimension_semantics=("arbitrary",) * len(grid), vmem_limit_bytes=VMEM_LIMIT
+        ),
+        cost_estimate=pl.CostEstimate(flops=flops, bytes_accessed=size, transcendentals=0),
+        name=name,
+    )(*[a for a, _ in ins])
+
+
+ROWS = 256
+
+
+def own_rows(steps, cols):
+    return pl.BlockSpec((ROWS, cols), lambda i: (jnp.minimum(i, steps - 1), 0))
+
+
+def partner_rows(steps, cols):
+    return pl.BlockSpec((ROWS, cols), lambda i: (jnp.maximum(i - steps, 0), 0))
+
+
+def pick_rows(i, steps, own_ref, partner_ref):
+    return jnp.where(i < steps, own_ref[...], partner_ref[...])
+
+
+def qkv_kernel(steps, groups, table, own, partner, first, second, mixed, weight, out_w, norms):
+    i = pl.program_id(0)
+    count, rows = first.shape[0], first.shape[1]
+    part = out_w.shape[2] // 2
+    cols = weight.shape[2]
+
+    @pl.when(i == 0)
+    def _():
+        for k in range(2 * count):
+            source = first if k < count else second
+            place = table[k % (2 * count)]
+            weight[place] = source[k % count, :, :cols]
+            norms[place] = source[k % count, :, cols + part :]
+            value = source[k % count, :, cols : cols + part]
+            for y in range(2):
+
+                @pl.when(lax.rem(place, 2) == y)
+                def _():
+                    out_w[lax.div(place, 2), :, y * part : (y + 1) * part] = value
+
+    rows_here = pick_rows(i, steps, own, partner)
+    for g in range(groups):
+        span = slice(g * cols // groups, (g + 1) * cols // groups)
+        tile = weight[:, :, span].reshape(2 * count * rows, cols // groups)
+        mixed[:, span] = dot(rows_here, tile).astype(BF16)
+
+
+def lane_masks():
+    lane = lax.broadcasted_iota(jnp.int32, (1, PAIR), 1)
+    return [lane < HEAD_DIM, lane >= HEAD_DIM]
+
+
+def keep(mask, value):
+    return jnp.where(mask, value, jnp.zeros_like(value))
+
+
+def fill_distance(distance):
+    row = lax.broadcasted_iota(jnp.int32, distance.shape, 0)
+    col = lax.broadcasted_iota(jnp.int32, distance.shape, 1)
+    distance[...] = jnp.abs(row - col).astype(F32)
+
+
+def scores_of(queries, keys, slope, distance):
+    raw = lax.dot_general(queries, keys, (((1,), (1,)), ((), ())), preferred_element_type=F32)
+    return raw - slope * distance
+
+
+def attend_kernel(flags, slopes, query, key, value, context, logs, distance):
+    block, pair = pl.program_id(0), pl.program_id(1)
+    masks = lane_masks()
+
+    @pl.when((block == 0) & (pair == 0))
+    def _():
+        fill_distance(distance)
+
+    def run(is_long):
+        keys_all, values_all = key[...], value[...]
+        for g in range(LONG // SHORT):
+            rows = slice(g * SHORT, (g + 1) * SHORT)
+            keys = keys_all if is_long else keys_all[rows]
+            values = values_all if is_long else values_all[rows]
+            away = distance[rows, :] if is_long else distance[:SHORT, :SHORT]
+            total = jnp.zeros((SHORT, PAIR), F32)
+            log_rows = []
+            for head in range(2):
+                q = keep(masks[head], query[rows, :]) * (HEAD_DIM**-0.5)
+                s = scores_of(q.astype(BF16), keys, slopes[pair * 2 + head], away)
+                top = jnp.max(s, axis=-1, keepdims=True)
+                e = jnp.exp(s - top)
+                norm = jnp.sum(e, axis=-1, keepdims=True)
+                p = (e * (1.0 / norm)).astype(BF16)
+                total = total + dot(p, keep(masks[head], values))
+                log_rows.append(top + jnp.log(norm))
+            context[rows, :] = total.astype(BF16)
+            logs[rows, :] = jnp.where(masks[0], log_rows[0], log_rows[1])
+
+    @pl.when(flags[block] > 0)
+    def _():
+        run(True)
+
+    @pl.when(flags[block] <= 0)
+    def _():
+        run(False)
+
+
+def attend_back_kernel(
+    blocks, flags, slopes, query, key, value, d_own, d_partner, logs, d_query, d_key, d_value, distance, key_t, value_t
+):
+    block, pair = pl.program_id(0), pl.program_id(1)
+    masks = lane_masks()
+    scale = HEAD_DIM**-0.5
+
+    @pl.when((block == 0) & (pair == 0))
+    def _():
+        fill_distance(distance)
+
+    def run(is_long):
+        keys_all, values_all = key[...], value[...]
+        for g in range(LONG // SHORT):
+            rows = slice(g * SHORT, (g + 1) * SHORT)
+            keys = keys_all if is_long else keys_all[rows]
+            values = values_all if is_long else values_all[rows]
+            away = distance[rows, :] if is_long else distance[:SHORT, :SHORT]
+            d_here = jnp.where(block == 0, d_own[rows, :], d_partner[rows, :])
+            d_q = jnp.zeros((SHORT, PAIR), F32)
+            d_k = jnp.zeros((PAIR, keys.shape[0]), F32)
+            d_v = jnp.zeros((PAIR, keys.shape[0]), F32)
+            for head in range(2):
+                q = (keep(masks[head], query[rows, :]) * scale).astype(BF16)
+                d_c = keep(masks[head], d_here)
+                s = scores_of(q, keys, slopes[pair * 2 + head], away)
+                log_row = logs[rows, head * HEAD_DIM : head * HEAD_DIM + 1]
+                p = jnp.exp(s - log_row)
+                d_p = lax.dot_general(d_c, values, (((1,), (1,)), ((), ())), preferred_element_type=F32)
+                d_s = (p * (d_p - jnp.sum(p * d_p, axis=-1, keepdims=True))).astype(BF16)
+                d_q = d_q + dot(d_s, (keep(masks[head], keys) * scale).astype(BF16))
+                d_k = d_k + dot(q.T, d_s)
+                d_v = d_v + dot(d_c.T, p.astype(BF16))
+            d_query[rows, :] = d_q.astype(BF16)
+            if not is_long:
+                d_key[rows, :] = d_k.T.astype(BF16)
+                d_value[rows, :] = d_v.T.astype(BF16)
+            elif g == 0:
+                key_t[...] = d_k
+                value_t[...] = d_v
+            else:
+                key_t[...] += d_k
+                value_t[...] += d_v
+        if is_long:
+            d_key[...] = key_t[...].T.astype(BF16)
+            d_value[...] = value_t[...].T.astype(BF16)
+
+    @pl.when(flags[block] > 0)
+    def _():
+        run(True)
+
+    @pl.when(flags[block] <= 0)
+    def _():
+        run(False)
+
+
+def spread(rows):
+    center = jnp.mean(rows, axis=-1, keepdims=True)
+    shifted = rows - center
+    inverse = lax.rsqrt(jnp.mean(shifted * shifted, axis=-1, keepdims=True) + 1e-05)
+    return shifted * inverse, inverse
+
+
+def norm_back(e, unit, inverse):
+    mean_e = jnp.mean(e, axis=-1, keepdims=True)
+    mean_en = jnp.mean(e * unit, axis=-1, keepdims=True)
+    return (e - mean_e - unit * mean_en) * inverse
+
+
+def first_norm_kernel(place, tokens, ctx_mine, ctx_other, w_mine, w_other, norms, weight, unit, inverse, low):
+    core = place[0]
+
+    @pl.when(pl.program_id(0) == 0)
+    def _():
+        for k in range(w_mine.shape[0]):
+            weight[2 * k + core] = w_mine[k]
+            weight[2 * k + 1 - core] = w_other[k]
+
+    half = weight.shape[0] // 2
+    mine = weight[pl.ds(core * half, half)].reshape(D // 2, D)
+    other = weight[pl.ds((1 - core) * half, half)].reshape(D // 2, D)
+    hidden = tokens[...].astype(F32) + (dot(ctx_mine[...], mine) + dot(ctx_other[...], other))
+    n, inv = spread(hidden)
+    unit[...] = n
+    inverse[...] = inv
+    low[...] = (n * norms[0:1, :] + norms[2:3, :]).astype(BF16)
+
+
+def gelu_parts(x):
+    t = 1.0 / (1.0 + (0.3275911 * 0.5**0.5) * jnp.abs(x))
+    poly = t * (
+        0.254829592 + t * (-0.284496736 + t * (1.421413741 + t * (-1.453152027 + t * 1.061405429)))
+    )
+    bell = jnp.exp(-0.5 * (x * x))
+    tail = 0.5 * poly * bell
+    phi = jnp.where(x >= 0, 1.0 - tail, tail)
+    return x * phi, phi + x * bell * 0.3989422804014327
+
+
+def fill_blocks(table, first, second, weight):
+    count = first.shape[0]
+    for k in range(2 * count):
+        weight[table[k]] = first[k] if k < count else second[k - count]
+
+
+def columns_of(weight, half, span):
+    count = weight.shape[0] // 2
+    return weight[half * count : (half + 1) * count, :, span].reshape(D, span.stop - span.start)
+
+
+def up_kernel(
+    steps, table, own, partner, gate_a, gate_b, value_a, value_b, product, active, slope, gate_w, value_w
+):
+    i = pl.program_id(0)
+
+    @pl.when(i == 0)
+    def _():
+        fill_blocks(table, gate_a, gate_b, gate_w)
+        fill_blocks(table, value_a, value_b, value_w)
+
+    rows = pick_rows(i, steps, own, partner)
+    width = gate_w.shape[2]
+    for half in range(2):
+        for start in range(0, width, 256):
+            span = slice(start, start + 256)
+            out = slice(half * width + start, half * width + start + 256)
+            gate = dot(rows, columns_of(gate_w, half, span))
+            up = dot(rows, columns_of(value_w, half, span))
+            act, grad = gelu_parts(gate)
+            product[:, out] = (act * up).astype(BF16)
+            active[:, out] = act.astype(BF16)
+            slope[:, out] = (up * grad).astype(BF16)
+
+
+def down_kernel(steps, table, product, down_a, down_b, own, partner, down_w):
+    i = pl.program_id(0)
+
+    @pl.when(i == 0)
+    def _():
+        fill_blocks(table, down_a, down_b, down_w)
+
+    width = down_w.shape[2]
+    total = 0.0
+    for half in range(2):
+        total = total + contract_cols(product[:, half * width : (half + 1) * width], columns_of(down_w, half, slice(0, width)))
+
+    @pl.when(i < steps)
+    def _():
+        own[...] = total
+
+    @pl.when(i >= steps)
+    def _():
+        partner[...] = total.astype(BF16)
+
+
+def second_norm_kernel(unit_one, norms, part_own, part_got, cotangent, out, d_z, d_ffn, sums):
+    normed = unit_one[...] * norms[0:1, :] + norms[2:3, :]
+    n, inv = spread(normed + (part_own[...] + part_got[...].astype(F32)))
+    gain = norms[1:2, :]
+    out[...] = (n * gain + norms[3:4, :]).astype(BF16)
+    c = cotangent[...].astype(F32)
+    back = norm_back(gain * c, n, inv)
+    d_z[...] = back
+    d_ffn[...] = back.astype(BF16)
+    add_sums(sums, c * n, c)
+
+
+def add_sums(sums, gain_terms, bias_terms):
+    @pl.when(pl.program_id(0) == 0)
+    def _():
+        sums[...] = jnp.zeros_like(sums)
+
+    sums[0:1, :] += jnp.sum(gain_terms, axis=0, keepdims=True)
+    sums[1:2, :] += jnp.sum(bias_terms, axis=0, keepdims=True)
+
+
+def ffn_back_kernel(
+    steps, own, partner, down_w, gate_w, value_w, active, slope, d_gate, d_up, back_own, back_partner
+):
+    i = pl.program_id(0)
+    rows = pick_rows(i, steps, own, partner)
+    width = down_w.shape[2]
+    total = jnp.zeros((ROWS, D), F32)
+    for half in range(2):
+        for start in range(0, width, 256):
+            span = slice(start, start + 256)
+            out = slice(half * width + start, half * width + start + 256)
+            d_product = dot(rows, columns_of(down_w, half, span))
+            dg = (d_product * slope[:, out].astype(F32)).astype(BF16)
+            du = (d_product * active[:, out].astype(F32)).astype(BF16)
+            d_gate[:, out] = dg
+            d_up[:, out] = du
+            total = total + contract_cols(dg, columns_of(gate_w, half, span))
+            total = total + contract_cols(du, columns_of(value_w, half, span))
+
+    @pl.when(i < steps)
+    def _():
+        back_own[...] = total
+
+    @pl.when(i >= steps)
+    def _():
+        back_partner[...] = total.astype(BF16)
+
+
+def weight_grad_kernel(per_half, table, left_own, left_partner, right, grad):
+    i = pl.program_id(0)
+    rows = left_own.shape[1]
+    value = dot(left_own[...], right[:rows, :]) + dot(left_partner[...], right[rows:, :])
+    value = value.astype(BF16)
+    count, tall = grad.shape[0] // 2, grad.shape[1]
+    half, start = lax.div(i, per_half), lax.rem(i, per_half) * 256
+    for k in range(count):
+        grad[table[half * count + k], :, pl.ds(pl.multiple_of(start, 256), 256)] = value[k * tall : (k + 1) * tall]
+
+
+def first_norm_back_kernel(
+    place,
+    unit_ref,
+    inverse,
+    norms,
+    d_z,
+    part_own,
+    part_got,
+    ctx_mine,
+    ctx_other,
+    weight,
+    d_hidden,
+    d_branch,
+    dctx_mine,
+    dctx_other,
+    grad,
+    sums,
+):
+    core = place[0]
+    unit = unit_ref[...]
+    d_normed = d_z[...] + (part_own[...] + part_got[...].astype(F32))
+    back = norm_back(norms[0:1, :] * d_normed, unit, inverse[...])
+    low = back.astype(BF16)
+    d_hidden[...] = back
+    d_branch[...] = low
+    add_sums(sums, d_normed * unit, d_normed)
+    half = weight.shape[0] // 2
+    dctx_mine[...] = contract_cols(low, weight[pl.ds(core * half, half)].reshape(D // 2, D)).astype(BF16)
+    dctx_other[...] = contract_cols(low, weight[pl.ds((1 - core) * half, half)].reshape(D // 2, D)).astype(BF16)
+
+    @pl.when(pl.program_id(0) == 0)
+    def _():
+        grad[...] = jnp.zeros_like(grad)
+
+    shape = (half,) + grad.shape[1:]
+    grad[pl.ds(core * half, half)] += dot(ctx_mine[...].T, low).reshape(shape)
+    grad[pl.ds((1 - core) * half, half)] += dot(ctx_other[...].T, low).reshape(shape)
+
+
+def qkv_grad_kernel(table, left_own, left_partner, d_query, d_key, d_value, out_grad, norm_grad, grad):
+    i = pl.program_id(0)
+    rows = left_own.shape[1]
+    count, tall = grad.shape[0], grad.shape[1]
+    cols = d_query.shape[1]
+    part = out_grad.shape[2] // 2
+    for g, right in enumerate((d_query, d_key, d_value)):
+
+        @pl.when(i == g)
+        def _():
+            value = (dot(left_own[...], right[:rows, :]) + dot(left_partner[...], right[rows:, :])).astype(BF16)
+            for k in range(count):
+                grad[table[k], :, g * cols : (g + 1) * cols] = value[k * tall : (k + 1) * tall]
+                if g == 0:
+                    y = k % 2
+                    grad[table[k], :, 3 * cols : 3 * cols + part] = out_grad[k // 2, :, y * part : (y + 1) * part]
+                    grad[table[k], :, 3 * cols + part :] = norm_grad[k]
+
+
+def input_grad_kernel(steps, d_query, d_key, d_value, weight, own, partner):
+    i = pl.program_id(0)
+    cols = d_query.shape[1]
+    total = 0.0
+    for g, left in enumerate((d_query, d_key, d_value)):
+        tile = weight[:, :, g * cols : (g + 1) * cols].reshape(D, cols)
+        total = total + contract_cols(left[...], tile)
+
+    @pl.when(i < steps)
+    def _():
+        own[...] = total
+
+    @pl.when(i >= steps)
+    def _():
+        partner[...] = total.astype(BF16)
+
+
+def by_core(core, mine, other, axis):
+    first = core == 0
+    return jnp.stack([jnp.where(first, mine, other), jnp.where(first, other, mine)], axis=axis)
+
+
+def half_of(core, halves, axis):
+    zero, one = (lax.index_in_dim(halves, k, axis, keepdims=False) for k in range(2))
+    first = core == 0
+    return jnp.where(first, zero, one), jnp.where(first, one, zero)
+
+
+def plane_shards(
+    wide,
+    narrow,
+    tokens,
+    w_qkv,
+    w_out,
+    w_gate,
+    w_value,
+    w_down,
+    norm_gains,
+    norm_biases,
+    long_count,
+    cotangent,
+):
+    plane = Plane(wide, narrow)
+    core, y_here = plane.core, plane.y
+    rows = tokens.shape[0]
+    steps = rows // ROWS
+    tall = w_qkv.shape[0]
+    blocks = wide * narrow // 2
+    z_size = plane.size["z"]
+    head_cols = D // 2
+    width = w_gate.shape[1] // 2
+    hidden = 2 * width
+    order = ("z", "a", "b")
+    qkv_to, qkv_from = plane.tables(order, lambda z, x, y: (z * 2 + x) * 2 + y)
+    ffn_to, ffn_from = plane.tables(order, lambda z, x, y: y * (2 * z_size) + z * 2 + x)
+    place = jnp.reshape(core, (1,)).astype(jnp.int32)
+
+    qkv_mine, qkv_other = half_of(core, w_qkv.reshape(tall, 3, 2, head_cols), 2)
+    norm_cols = jnp.concatenate([norm_gains, norm_biases], axis=0).T
+    norm_cols = jnp.pad(norm_cols, ((0, 0), (0, 128 - norm_cols.shape[1])))
+    head_part = jnp.concatenate([qkv_mine.reshape(tall, 3 * head_cols), norm_cols], axis=1)
+    head_send = jnp.concatenate([qkv_other.reshape(tall, 3 * head_cols), norm_cols], axis=1)
+    head_got = plane.swap(head_send, "core")
+    tokens_other = plane.swap(tokens, "core")
+    head_part = jnp.where(y_here == core, head_part, head_got)
+    out_cols = lax.dynamic_slice_in_dim(w_out, y_here * (D // narrow), D // narrow, axis=1)
+    head_part = jnp.concatenate(
+        [head_part[:, : 3 * head_cols], out_cols, head_part[:, 3 * head_cols :]], axis=1
+    )
+    qkv_blocks = plane.gather(head_part, order)
+
+    ffn_parts = jnp.stack([w_gate, w_value, w_down.T], axis=0).reshape(3, tall, 2, width)
+    ffn_mine, ffn_other = half_of(core, ffn_parts, 2)
+    ffn_got = plane.swap(ffn_other, "core")
+    ffn_chip = by_core(core, ffn_mine, ffn_got, 1).reshape(3, 2 * tall, width)
+    gate_blocks = plane.gather(ffn_chip[0], order)
+    value_blocks = plane.gather(ffn_chip[1], order)
+    down_blocks = plane.gather(ffn_chip[2], order)
+
+    flag = jnp.broadcast_to(long_count.astype(F32), (8, 128))
+    flags = jnp.stack([long_count[0, 0], plane.swap(flag, "core")[0, 0].astype(jnp.int32)])
+    slopes = lax.dynamic_slice_in_dim(alibi_slopes(HEADS), core * (HEADS // 2), HEADS // 2)
+
+    half_blocks = blocks // 2
+    piece = qkv_blocks[0].shape
+    mixed, qkv_w, out_mine, norm_table = kernel_call(
+        functools.partial(qkv_kernel, steps, 3),
+        (2 * steps,),
+        [
+            (qkv_to, smem()),
+            (tokens, own_rows(steps, D)),
+            (tokens_other, partner_rows(steps, D)),
+            (qkv_blocks[0], whole(piece)),
+            (qkv_blocks[1], whole(piece)),
+        ],
+        [
+            ((2 * rows, 3 * head_cols), BF16, pl.BlockSpec((ROWS, 3 * head_cols), lambda i: (i, 0))),
+            ((blocks, tall, 3 * head_cols), BF16, whole((blocks, tall, 3 * head_cols))),
+            ((half_blocks, tall, D), BF16, whole((half_blocks, tall, D))),
+            ((blocks, tall, 128), BF16, whole((blocks, tall, 128))),
+        ],
+        flops=2 * 2 * rows * D * 3 * head_cols,
+        name="mixed",
+    )
+    out_other = plane.swap(out_mine, "core")
+    norms = norm_table.reshape(D, 128)[:, :4].T.astype(F32)
+    norms = jnp.stack([norms[0], norms[1], norms[2], norms[3]])
+
+    pairs = head_cols // PAIR
+
+    def head_block(first):
+        return pl.BlockSpec((rows, PAIR), lambda b, p: (b, first + p))
+
+    context, logs = kernel_call(
+        attend_kernel,
+        (2, pairs),
+        [
+            (flags, smem()),
+            (slopes, smem()),
+            (mixed, head_block(0)),
+            (mixed, head_block(pairs)),
+            (mixed, head_block(2 * pairs)),
+        ],
+        [
+            ((2 * rows, head_cols), BF16, head_block(0)),
+            ((2 * rows, head_cols), F32, head_block(0)),
+        ],
+        scratch=[pltpu.VMEM((LONG, LONG), F32)],
+        flops=4 * 2 * rows * LONG * D,
+        name="attend",
+    )
+    ctx_mine = context[:rows]
+    ctx_other = plane.swap(context[rows:], "core")
+
+    def step_rows(cols):
+        return pl.BlockSpec((ROWS, cols), lambda i: (i, 0))
+
+    out_w, unit_one, inverse_one, low = kernel_call(
+        first_norm_kernel,
+        (steps,),
+        [
+            (place, smem()),
+            (tokens, step_rows(D)),
+            (ctx_mine, step_rows(head_cols)),
+            (ctx_other, step_rows(head_cols)),
+            (out_mine, whole(out_mine.shape)),
+            (out_other, whole(out_mine.shape)),
+            (norms, whole(norms.shape)),
+        ],
+        [
+            ((blocks, tall, D), BF16, whole((blocks, tall, D))),
+            ((rows, D), F32, step_rows(D)),
+            ((rows, 1), F32, step_rows(1)),
+            ((rows, D), BF16, step_rows(D)),
+        ],
+        flops=2 * rows * D * D,
+        name="first_norm",
+    )
+    low_other = plane.swap(low, "core")
+
+    w_shape = (blocks, 2 * tall, width)
+    product, active, slope, gate_w, value_w = kernel_call(
+        functools.partial(up_kernel, steps),
+        (2 * steps,),
+        [
+            (ffn_to, smem()),
+            (low, own_rows(steps, D)),
+            (low_other, partner_rows(steps, D)),
+        ]
+        + [(part, whole(part.shape)) for part in gate_blocks + value_blocks],
+        [((2 * rows, hidden), BF16, step_rows(hidden))] * 3 + [(w_shape, BF16, whole(w_shape))] * 2,
+        flops=2 * 2 * rows * D * 2 * hidden,
+        name="up",
+    )
+    part_own, part_send, down_w = kernel_call(
+        functools.partial(down_kernel, steps),
+        (2 * steps,),
+        [(ffn_to, smem()), (product, step_rows(hidden))] + [(part, whole(part.shape)) for part in down_blocks],
+        [
+            ((rows, D), F32, own_rows(steps, D)),
+            ((rows, D), BF16, partner_rows(steps, D)),
+            (w_shape, BF16, whole(w_shape)),
+        ],
+        flops=2 * 2 * rows * D * hidden,
+        name="down",
+    )
+    part_got = plane.swap(part_send, "core")
+    layer_out, d_z, d_ffn, sums_two = kernel_call(
+        second_norm_kernel,
+        (steps,),
+        [
+            (unit_one, step_rows(D)),
+            (norms, whole(norms.shape)),
+            (part_own, step_rows(D)),
+            (part_got, step_rows(D)),
+            (cotangent, step_rows(D)),
+        ],
+        [
+            ((rows, D), BF16, step_rows(D)),
+            ((rows, D), F32, step_rows(D)),
+            ((rows, D), BF16, step_rows(D)),
+            ((8, D), F32, whole((8, D))),
+        ],
+        name="second_norm",
+    )
+    d_ffn_other = plane.swap(d_ffn, "core")
+
+    def weight_grad(left, left_other, right):
+        return kernel_call(
+            functools.partial(weight_grad_kernel, width // 256),
+            (hidden // 256,),
+            [
+                (ffn_from, smem()),
+                (left.T, whole((D, rows))),
+                (left_other.T, whole((D, rows))),
+                (right, pl.BlockSpec((2 * rows, 256), lambda i: (0, i))),
+            ],
+            [(w_shape, BF16, whole(w_shape))],
+            flops=2 * 2 * rows * D * hidden,
+            name="weight_grad",
+        )[0]
+
+    grad_down = plane.reduce(weight_grad(d_ffn, d_ffn_other, product), order)
+    d_gate, d_up, back_own, back_send = kernel_call(
+        functools.partial(ffn_back_kernel, steps),
+        (2 * steps,),
+        [
+            (d_ffn, own_rows(steps, D)),
+            (d_ffn_other, partner_rows(steps, D)),
+            (down_w, whole(w_shape)),
+            (gate_w, whole(w_shape)),
+            (value_w, whole(w_shape)),
+            (active, step_rows(hidden)),
+            (slope, step_rows(hidden)),
+        ],
+        [((2 * rows, hidden), BF16, step_rows(hidden))] * 2
+        + [((rows, D), F32, own_rows(steps, D)), ((rows, D), BF16, partner_rows(steps, D))],
+        flops=3 * 2 * 2 * rows * D * hidden,
+        name="ffn_back",
+    )
+    back_got = plane.swap(back_send, "core")
+    grad_gate = plane.reduce(weight_grad(low, low_other, d_gate), order)
+    grad_value = plane.reduce(weight_grad(low, low_other, d_up), order)
+
+    d_hidden, d_branch, dctx_mine, dctx_send, out_grad, sums_one = kernel_call(
+        first_norm_back_kernel,
+        (steps,),
+        [
+            (place, smem()),
+            (unit_one, step_rows(D)),
+            (inverse_one, step_rows(1)),
+            (norms, whole(norms.shape)),
+            (d_z, step_rows(D)),
+            (back_own, step_rows(D)),
+            (back_got, step_rows(D)),
+            (ctx_mine, step_rows(head_cols)),
+            (ctx_other, step_rows(head_cols)),
+            (out_w, whole(out_w.shape)),
+        ],
+        [
+            ((rows, D), F32, step_rows(D)),
+            ((rows, D), BF16, step_rows(D)),
+            ((rows, head_cols), BF16, step_rows(head_cols)),
+            ((rows, head_cols), BF16, step_rows(head_cols)),
+            ((blocks, tall, D), F32, whole((blocks, tall, D))),
+            ((8, D), F32, whole((8, D))),
+        ],
+        flops=2 * 2 * rows * D * D,
+        name="first_norm_back",
+    )
+    dctx_got = plane.swap(dctx_send, "core")
+    out_keep, out_send = half_of(core, out_grad.reshape(half_blocks, 2, tall, D), 1)
+    out_sum = (out_keep + plane.swap(out_send.astype(BF16), "core").astype(F32)).astype(BF16)
+    sums = jnp.stack([sums_one[0], sums_two[0], sums_one[1], sums_two[1]], axis=1)
+    norm_grad = jnp.pad(sums, ((0, 0), (0, 124))).astype(BF16).reshape(blocks, tall, 128)
+
+    def whole_pair(first):
+        return pl.BlockSpec((rows, PAIR), lambda b, p: (0, first + p))
+
+    d_query, d_key, d_value = kernel_call(
+        functools.partial(attend_back_kernel, 2),
+        (2, pairs),
+        [
+            (flags, smem()),
+            (slopes, smem()),
+            (mixed, head_block(0)),
+            (mixed, head_block(pairs)),
+            (mixed, head_block(2 * pairs)),
+            (dctx_mine, whole_pair(0)),
+            (dctx_got, whole_pair(0)),
+            (logs, head_block(0)),
+        ],
+        [((2 * rows, head_cols), BF16, head_block(0))] * 3,
+        scratch=[
+            pltpu.VMEM((LONG, LONG), F32),
+            pltpu.VMEM((PAIR, LONG), F32),
+            pltpu.VMEM((PAIR, LONG), F32),
+        ],
+        flops=10 * 2 * rows * LONG * D,
+        name="attend_back",
+    )
+    grad_shape = (blocks, tall, 3 * head_cols + D // 2 + 128)
+    parts = [(v, whole((2 * rows, head_cols))) for v in (d_query, d_key, d_value)]
+    grad_head = kernel_call(
+        qkv_grad_kernel,
+        (3,),
+        [
+            (qkv_from, smem()),
+            (tokens.T, whole((D, rows))),
+            (tokens_other.T, whole((D, rows))),
+        ]
+        + parts
+        + [(out_sum, whole(out_sum.shape)), (norm_grad, whole(norm_grad.shape))],
+        [(grad_shape, BF16, whole(grad_shape))],
+        flops=2 * 2 * rows * D * 3 * head_cols,
+        name="qkv_grad",
+    )[0]
+    head_sum = plane.reduce(grad_head, order).astype(BF16)
+    in_own, in_send = kernel_call(
+        functools.partial(input_grad_kernel, steps),
+        (2 * steps,),
+        [(v, step_rows(head_cols)) for v in (d_query, d_key, d_value)] + [(qkv_w, whole(qkv_w.shape))],
+        [((rows, D), F32, own_rows(steps, D)), ((rows, D), BF16, partner_rows(steps, D))],
+        flops=2 * 2 * rows * D * 3 * head_cols,
+        name="input_grad",
+    )
+    input_grad = d_hidden + in_own + plane.swap(in_send, "core").astype(F32)
+
+    def ffn_piece(total):
+        mine, other = half_of(core, total.astype(BF16).reshape(2, tall, width), 0)
+        return by_core(core, mine, plane.swap(other, "core"), 1).reshape(tall, 2 * width).astype(F32)
+
+    gate_piece, value_piece = ffn_piece(grad_gate), ffn_piece(grad_value)
+    down_piece = ffn_piece(grad_down).T
+    both = by_core(y_here, head_sum, plane.swap(head_sum, "y"), 0)
+    out_piece = both[:, :, 3 * head_cols : 3 * head_cols + D // 2]
+    out_piece = jnp.transpose(out_piece, (1, 0, 2)).reshape(tall, D).astype(F32)
+    rest = jnp.concatenate([both[:, :, : 3 * head_cols], both[:, :, 3 * head_cols + D // 2 :]], axis=2)
+    mine, other = half_of(core, rest, 0)
+    got = plane.swap(other, "core")
+    qkv_piece = by_core(
+        core, mine[:, : 3 * head_cols].reshape(tall, 3, head_cols), got[:, : 3 * head_cols].reshape(tall, 3, head_cols), 2
+    )
+    qkv_piece = qkv_piece.reshape(tall, 6 * head_cols).astype(F32)
+    norm_piece = (mine[:, 3 * head_cols : 3 * head_cols + 4].astype(F32) + got[:, 3 * head_cols : 3 * head_cols + 4].astype(F32)).T
+    return (
+        layer_out,
+        input_grad,
+        qkv_piece,
+        out_piece,
+        gate_piece,
+        value_piece,
+        down_piece,
+        norm_piece[:2],
+        norm_piece[2:],
+    )
+
+
 def solution(mesh):
+    wide, narrow = mesh.shape["wide"], mesh.shape["narrow"]
     placed = (
         P(("wide", "narrow"), None),
         P("wide", None),
@@ -257,8 +1105,12 @@
         P("wide", "narrow"),
         P(("wide", "narrow"), None),
     )
+    if narrow == 2 and wide % 16 == 0 and D % (16 * wide) == 0:
+        body = functools.partial(plane_shards, wide, narrow)
+    else:
+        body = general_shards
     return jax.shard_map(
-        shards,
+        body,
         mesh=mesh,
         in_specs=placed,
         out_specs=(

time: 900 us -> 365 us (0.41)
  waiting for transfers between devices: 648 us -> 92.9 us
  Pallas kernels: 0 us -> 129 us
  matrix products: 124 us -> 0 us
  starting transfers between devices: 1.77 us -> 77.5 us
  blocking collectives: 44.5 us -> 0 us
  local copies, waits for them, and re-layouts: 25.6 us -> 48.3 us
  other arithmetic: 32.7 us -> 15 us
  between operations: 15 us -> 2.87 us
    reduce_scatter x6 -> x0, waiting for transfers between devices: 261 us -> none  [the longest x1 64.7 us: shards(): lax.psum_scatter(grad_gate.astype(jnp.bfloat16), 'wide', scatter_dimensio...]
    unnamed x20 -> x0, waiting for transfers between devices: 180 us -> none
    all_gather x7 -> x0, waiting for transfers between devices: 177 us -> none  [the longest x1 37.7 us: shards(): lax.all_gather(w_gate, 'wide', axis=0, tiled=True)]
    pallas_call x0 -> x14, Pallas kernels: none -> 129 us  [kernel_call(): pl.pallas_call(body, grid=grid, in_specs=[spec for _, spec in ins], out_s...]
    dot_general x22 -> x0, matrix products: 124 us -> none  [the longest x5 27.3 us: contract_rows(): lax.dot_general(left, right, (((0,), (0,)), ((), ())), preferred_element_...]
    ppermute x0 -> x58, waiting for transfers between devices: none -> 92.9 us  [swap(): return lax.ppermute(value, AXES, self.pairs[dim, step])]
    ppermute x0 -> x58, starting transfers between devices: none -> 77.5 us  [swap(): return lax.ppermute(value, AXES, self.pairs[dim, step])]
    all_gather x2 -> x0, blocking collectives: 40.8 us -> none  [the longest x1 23.2 us: shards(): lax.all_gather(norm_gains, 'wide', axis=1, tiled=True)]
  transfers between devices with their start and end apart: 17 -> 58, of which waited for: 17 -> 18; matrix products, arithmetic and copies ran while one was open for 16% -> 13% of each run, Pallas kernels for 0% -> 27%
where the time goes in v1:
time: 365 us
  Pallas kernels  129 us (35%)
  waiting for transfers between devices  92.9 us (25%)
  starting transfers between devices  77.5 us (21%)
  local copies, waits for them, and re-layouts  48.3 us (13%)
  other arithmetic  15 us (4%)
    pallas_call x14, Pallas kernels, kernel_call(): pl.pallas_call(body, grid=grid, in_specs=[spec for _, spec in ins], out_s...  129 us
    ppermute x58, waiting for transfers between devices, swap(): return lax.ppermute(value, AXES, self.pairs[dim, step])  92.9 us
    ppermute x58, starting transfers between devices, swap(): return lax.ppermute(value, AXES, self.pairs[dim, step])  77.5 us
    unnamed x100, local copies, waits for them, and re-layouts  16.7 us
    slice x12, local copies, waits for them, and re-layouts, reduce(): got = [self.swap(blocks[k], dim, k) for k in range(1, size)]  9.73 us
  transfers between devices with their start and end apart: 58, of which 18 were waited for; matrix products, arithmetic and copies ran while one was open for 13% of the time, Pallas kernels for 27%

profile of v1, /device:TPU:1, one launch (start us, length us, event | category | flops | bytes accessed | tf_op | source)
XLA Modules:
  0.0 365.1 jit_solution(9809882488802559112)
XLA Ops:
  8.7 4.6 %collective-permute-start.5 = (bf16[1,48,1664]{2,1,0:T(8,128)(2,1)S(1)}, bf16[1,48,1664]{2,1,0:T(8,128)(2,1)S(1)}, u32[]{:S(2)}, u32[]{:S(2)}) collective-permute-start(bf16[1,48,1664]{2,1,0:T(8,128)(2,1)S(1)} %maximum_bitcast_fusion), channel_id=1, source_target_pairs={{0,24},{1,25},{2,26},{3,27},{4,28},{5,29},{6,30},{7,31},{8,16},{9,... | collective-permute-start | bytes 479240 | tf_op jit(solution)/shard_map/ppermute | solution.py:289
  14.4 3.2 collective-permute-start.14
  18.5 6.1 %collective-permute-start.23 = (bf16[1,96,768]{2,1,0:T(8,128)(2,1)S(1)}, bf16[1,96,768]{2,1,0:T(8,128)(2,1)S(1)}, u32[]{:S(2)}, u32[]{:S(2)}) collective-permute-start(bf16[1,96,768]{2,1,0:T(8,128)(2,1)S(1)} %bitcast.159), channel_id=1, source_target_pairs={{0,16},{1,17},{2,18},{3,19},{4,20},{5,21},{6,22},{7,23},{8,24},{9,... | collective-permute-start | bytes 442376 | tf_op jit(solution)/shard_map/ppermute | solution.py:289
  24.6 11.6 %collective-permute-done.4 = bf16[1,48,1664]{2,1,0:T(8,128)(2,1)S(1)} collective-permute-done((bf16[1,48,1664]{2,1,0:T(8,128)(2,1)S(1)}, bf16[1,48,1664]{2,1,0:T(8,128)(2,1)S(1)}, u32[]{:S(2)}, u32[]{:S(2)}) %collective-permute-start.4) | collective-permute-done | bytes 159776 | tf_op jit(solution)/shard_map/ppermute | solution.py:289
  36.3 1.3 collective-permute-start.6
  39.6 4.2 %collective-permute-start.13 = (bf16[1,96,768]{2,1,0:T(8,128)(2,1)S(1)}, bf16[1,96,768]{2,1,0:T(8,128)(2,1)S(1)}, u32[]{:S(2)}, u32[]{:S(2)}) collective-permute-start(bf16[1,96,768]{2,1,0:T(8,128)(2,1)S(1)} %bitcast.154), channel_id=1, source_target_pairs={{0,16},{1,17},{2,18},{3,19},{4,20},{5,21},{6,22},{7,23},{8,24},{9,... | collective-permute-start | bytes 442376 | tf_op jit(solution)/shard_map/ppermute | solution.py:289
  43.8 1.9 collective-permute-done.23
  45.7 2.2 collective-permute-start.19
  50.3 3.8 %collective-permute-done.13 = bf16[1,96,768]{2,1,0:T(8,128)(2,1)S(1)} collective-permute-done((bf16[1,96,768]{2,1,0:T(8,128)(2,1)S(1)}, bf16[1,96,768]{2,1,0:T(8,128)(2,1)S(1)}, u32[]{:S(2)}, u32[]{:S(2)}) %collective-permute-start.13) | collective-permute-done | bytes 147488 | tf_op jit(solution)/shard_map/ppermute | solution.py:289
  54.0 3.2 collective-permute-start.1
  59.4 1.2 collective-permute-start.15
  60.6 4.0 %collective-permute-done.18 = bf16[1,96,768]{2,1,0:T(8,128)(2,1)S(1)} collective-permute-done((bf16[1,96,768]{2,1,0:T(8,128)(2,1)S(1)}, bf16[1,96,768]{2,1,0:T(8,128)(2,1)S(1)}, u32[]{:S(2)}, u32[]{:S(2)}) %collective-permute-start.18) | collective-permute-done | bytes 147488 | tf_op jit(solution)/shard_map/ppermute | solution.py:289
  72.3 22.5 %collective-permute-done.20 = bf16[4,96,768]{2,1,0:T(8,128)(2,1)} collective-permute-done((bf16[4,96,768]{2,1,0:T(8,128)(2,1)}, bf16[4,96,768]{2,1,0:T(8,128)(2,1)}, u32[]{:S(2)}, u32[]{:S(2)}) %collective-permute-start.20) | collective-permute-done | bytes 589856 | tf_op jit(solution)/shard_map/ppermute | solution.py:289
  94.8 1.9 constant_dynamic-update-slice_fusion.10.value_a
  97.0 7.1 %mixed.1 = (bf16[1024,1152]{1,0:T(8,128)(2,1)}, bf16[16,48,1152]{2,1,0:T(8,128)(2,1)}, bf16[8,48,768]{2,1,0:T(8,128)(2,1)}, bf16[16,48,128]{2,1,0:T(8,128)(2,1)}) custom-call(s32[16]{0:T(128)} %get-tuple-element.171.table, bf16[512,768]{1,0:T(8,128)(2,1)} %tokens.1, bf16[512,768]{1,0:T(8,128)(2,1)} %copy.139.partner, ...), custom_call_target="tpu_custom_call" | custom-call | flops 1811939328 | bytes 9044032 | tf_op jit(solution)/shard_map/mixed/pallas_call | solution.py:348
  104.0 13.4 %attend.1 = (bf16[1024,384]{1,0:T(8,128)(2,1)}, f32[1024,384]{1,0:T(8,128)}) custom-call(s32[2]{0:T(128)} %pad_add_fusion.flags, f32[6]{0:T(128)} %dynamic_slice.6.slopes, bf16[1024,1152]{1,0:T(8,128)(2,1)} %get-tuple-element.45.query.key.value, bf16[1024,1152]{1,0:T(8,128)(2,1)} %get-tuple-element.45.query.key.value, ...), custom_call_target="tpu_custom_call" | custom-call | flops 1610612736 | bytes 9437216 | tf_op jit(solution)/shard_map/attend/pallas_call | solution.py:348
  117.4 2.0 fusion.32
  119.9 1.9 constant_dynamic-update-slice_fusion.5.gate_a
  124.2 4.5 %first_norm.1 = (bf16[16,48,768]{2,1,0:T(8,128)(2,1)}, f32[512,768]{1,0:T(8,128)}, f32[512,1]{1,0:T(8,128)}, bf16[512,768]{1,0:T(8,128)(2,1)}) custom-call(s32[1]{0:T(128)} %bitcast.place, bf16[512,768]{1,0:T(8,128)(2,1)} %tokens.1, bf16[512,384]{1,0:T(8,128)(2,1)} %get-tuple-element.127.ctx_mine, bf16[512,384]{1,0:T(8,128)(2,1)} %copy-done.10, ...), custom_call_target="tpu_custom_call" | custom-call | flops 603979776 | bytes 6305796 | tf_op jit(solution)/shard_map/first_norm/pallas_call | solution.py:348
  128.8 1.4 copy.141
  131.3 3.9 %collective-permute-start.26 = (bf16[8,96,768]{2,1,0:T(8,128)(2,1)}, bf16[8,96,768]{2,1,0:T(8,128)(2,1)S(1)}, u32[]{:S(2)}, u32[]{:S(2)}) collective-permute-start(bf16[8,96,768]{2,1,0:T(8,128)(2,1)} %constant_dynamic-update-slice_fusion.15.down_a), channel_id=1, source_target_pairs={{0,1},{1,0},{2,6},{3,7},{4,5},{5,4},{6,2},{7,3},{8,9},{9,8},{10,14... | collective-permute-start | bytes 3538952 | tf_op jit(solution)/shard_map/ppermute | solution.py:289
  137.5 13.4 %up.1 = (bf16[1024,1536]{1,0:T(8,128)(2,1)}, bf16[1024,1536]{1,0:T(8,128)(2,1)}, bf16[1024,1536]{1,0:T(8,128)(2,1)}, bf16[16,96,768]{2,1,0:T(8,128)(2,1)}, bf16[16,96,768]{2,1,0:T(8,128)(2,1)}) custom-call(s32[16]{0:T(128)} %get-tuple-element.172.table, bf16[512,768]{1,0:T(8,128)(2,1)} %get-tuple-element.50.own, bf16[512,768]{1,0:T(8,128)(2,1)} %copy.146.partner, ...), custom_call_target="tpu_custom_call" | custom-call | flops 4831838208 | bytes 20447296 | tf_op jit(solution)/shard_map/up/pallas_call | solution.py:348
  152.0 7.9 %down.1 = (f32[512,768]{1,0:T(8,128)}, bf16[512,768]{1,0:T(8,128)(2,1)}, bf16[16,96,768]{2,1,0:T(8,128)(2,1)}) custom-call(s32[16]{0:T(128)} %get-tuple-element.172.table, bf16[1024,1536]{1,0:T(8,128)(2,1)} %get-tuple-element.51.product.right, bf16[8,96,768]{2,1,0:T(8,128)(2,1)} %constant_dynamic-update-slice_fusion.15.down_a, bf16[8,96,768]{2,1,0:T(8,128)(2,1)} %copy-done.35), custom_call_target="tpu_custom_call" | custom-call | flops 2415919104 | bytes 10223680 | tf_op jit(solution)/shard_map/down/pallas_call | solution.py:348
  160.8 2.1 collective-permute-done.27.part_got
  163.9 4.3 %second_norm.1 = (bf16[512,768]{1,0:T(8,128)(2,1)}, f32[512,768]{1,0:T(8,128)}, bf16[512,768]{1,0:T(8,128)(2,1)}, f32[8,768]{1,0:T(8,128)}) custom-call(f32[512,768]{1,0:T(8,128)} %get-tuple-element.49.unit_one.unit_ref, f32[4,768]{1,0:T(4,128)} %bitcast.178, f32[512,768]{1,0:T(8,128)} %get-tuple-element.52.part_own, bf16[512,768]{1,0:T(8,128)(2,1)} %copy-done.18, ...), custom_call_target="tpu_custom_call" | custom-call | bytes 7901184 | tf_op jit(solution)/shard_map/second_norm/pallas_call | solution.py:348
  168.2 1.4 copy.147
  170.1 1.9 collective-permute-done.28
  173.2 18.7 %ffn_back.1 = (bf16[1024,1536]{1,0:T(8,128)(2,1)}, bf16[1024,1536]{1,0:T(8,128)(2,1)}, f32[512,768]{1,0:T(8,128)}, bf16[512,768]{1,0:T(8,128)(2,1)}) custom-call(bf16[512,768]{1,0:T(8,128)(2,1)} %get-tuple-element.57.own, bf16[512,768]{1,0:T(8,128)(2,1)} %copy.148.partner, bf16[16,96,768]{2,1,0:T(8,128)(2,1)} %get-tuple-element.58.down_w, ...), custom_call_target="tpu_custom_call" | custom-call | flops 7247757312 | bytes 23592960 | tf_op jit(solution)/shard_map/ffn_back/pallas_call | solution.py:348
  192.3 7.5 %weight_grad.5 = bf16[16,96,768]{2,1,0:T(8,128)(2,1)} custom-call(s32[16]{0:T(128)} %get-tuple-element.169.table, bf16[768,512]{1,0:T(8,128)(2,1)} %bitcast.166, bf16[768,512]{1,0:T(8,128)(2,1)} %bitcast.167, bf16[1024,1536]{1,0:T(8,128)(2,1)} %get-tuple-element.51.product.right), custom_call_target="tpu_custom_call" | custom-call | flops 2415919104 | bytes 7077952 | tf_op jit(solution)/shard_map/weight_grad/pallas_call | solution.py:348
  199.8 2.4 slice.391
  202.2 2.1 collective-permute-start.52
  204.3 7.5 %weight_grad.4 = bf16[16,96,768]{2,1,0:T(8,128)(2,1)} custom-call(s32[16]{0:T(128)} %get-tuple-element.169.table, bf16[768,512]{1,0:T(8,128)(2,1)} %bitcast.162, bf16[768,512]{1,0:T(8,128)(2,1)} %bitcast.164, bf16[1024,1536]{1,0:T(8,128)(2,1)} %get-tuple-element.80.right), custom_call_target="tpu_custom_call" | custom-call | flops 2415919104 | bytes 7077952 | tf_op jit(solution)/shard_map/weight_grad/pallas_call | solution.py:348
  211.8 2.4 slice.381
  214.1 7.4 %weight_grad.3 = bf16[16,96,768]{2,1,0:T(8,128)(2,1)} custom-call(s32[16]{0:T(128)} %get-tuple-element.169.table, bf16[768,512]{1,0:T(8,128)(2,1)} %bitcast.163, bf16[768,512]{1,0:T(8,128)(2,1)} %bitcast.165, bf16[1024,1536]{1,0:T(8,128)(2,1)} %get-tuple-element.79.right), custom_call_target="tpu_custom_call" | custom-call | flops 2415919104 | bytes 7077952 | tf_op jit(solution)/shard_map/weight_grad/pallas_call | solution.py:348
  221.6 2.4 slice.371
  224.0 1.5 collective-permute-start.46
  226.4 7.6 %first_norm_back.1 = (f32[512,768]{1,0:T(8,128)}, bf16[512,768]{1,0:T(8,128)(2,1)}, bf16[512,384]{1,0:T(8,128)(2,1)}, bf16[512,384]{1,0:T(8,128)(2,1)}, f32[16,48,768]{2,1,0:T(8,128)}, /*index=5*/f32[8,768]{1,0:T(8,128)}) custom-call(s32[1]{0:T(128)} %bitcast.place, f32[512,768]{1,0:T(8,128)} %get-tuple-element.49.unit_one.unit_ref, ...), custom_call_target="tpu_custom_call" | custom-call | flops 1207959552 | bytes 13015044 | tf_op jit(solution)/shard_map/first_norm_back/pallas_call | solution.py:348
  234.7 2.6 fusion.1
  239.1 15.4 %attend_back.1 = (bf16[1024,384]{1,0:T(8,128)(2,1)}, bf16[1024,384]{1,0:T(8,128)(2,1)}, bf16[1024,384]{1,0:T(8,128)(2,1)}) custom-call(s32[2]{0:T(128)} %pad_add_fusion.flags, f32[6]{0:T(128)} %dynamic_slice.6.slopes, bf16[1024,1152]{1,0:T(8,128)(2,1)} %get-tuple-element.45.query.key.value, bf16[1024,1152]{1,0:T(8,128)(2,1)} %get-tuple-element.45.query.key.value, ...), custom_call_target="tpu_custom_call" | custom-call | flops 4026531840 | bytes 11796512 | tf_op jit(solution)/shard_map/attend_back/pallas_call | solution.py:348
  254.5 6.9 %input_grad.1 = (f32[512,768]{1,0:T(8,128)}, bf16[512,768]{1,0:T(8,128)(2,1)}) custom-call(bf16[1024,384]{1,0:T(8,128)(2,1)} %get-tuple-element.70.d_query, bf16[1024,384]{1,0:T(8,128)(2,1)} %get-tuple-element.71.d_key, bf16[1024,384]{1,0:T(8,128)(2,1)} %get-tuple-element.72.d_value, bf16[16,48,1152]{2,1,0:T(8,128)(2,1)} %get-tuple-element.73.weight), custom_call_target="tpu_custom_call" | custom-call | flops 1811939328 | bytes 6488064 | tf_op jit(solution)/shard_map/input_grad/pallas_call | solution.py:348
  263.8 1.8 add_convert_fusion.3
  268.2 2.1 fusion.out_grad
  270.3 6.8 %qkv_grad.1 = bf16[16,48,1664]{2,1,0:T(8,128)(2,1)} custom-call(s32[16]{0:T(128)} %get-tuple-element.170.table, bf16[768,512]{1,0:T(8,128)(2,1)} %bitcast.145, bf16[768,512]{1,0:T(8,128)(2,1)} %bitcast.146, bf16[1024,384]{1,0:T(8,128)(2,1)} %get-tuple-element.70.d_query, bf16[1024,384]{1,0:T(8,128)(2,1)} %get-tuple-element.71.d_key, ...), custom_call_target="tpu_custom_call" | custom-call | flops 1811939328 | bytes 7274560 | tf_op jit(solution)/shard_map/qkv_grad/pallas_call | solution.py:348
  277.1 1.4 slice.355
  278.5 4.2 %collective-permute-start.33 = (bf16[8,48,1664]{2,1,0:T(8,128)(2,1)S(1)}, bf16[8,48,1664]{2,1,0:T(8,128)(2,1)S(1)}, u32[]{:S(2)}, u32[]{:S(2)}) collective-permute-start(bf16[8,48,1664]{2,1,0:T(8,128)(2,1)S(1)} %slice.355), channel_id=1, source_target_pairs={{0,1},{1,0},{2,6},{3,7},{4,5},{5,4},{6,2},{7,3},{8,9},{9,8},{10,14... | collective-permute-start | bytes 3833864 | tf_op jit(solution)/shard_map/ppermute | solution.py:289
  283.2 2.2 collective-permute-done.47
  285.4 1.7 collective-permute-start.55
  287.6 3.0 collective-permute-start.42
  290.6 2.2 collective-permute-start.44
  292.8 5.9 %collective-permute-done.55 = bf16[1,96,768]{2,1,0:T(8,128)(2,1)S(1)} collective-permute-done((bf16[1,96,768]{2,1,0:T(8,128)(2,1)S(1)}, bf16[1,96,768]{2,1,0:T(8,128)(2,1)S(1)}, u32[]{:S(2)}, u32[]{:S(2)}) %collective-permute-start.55) | collective-permute-done | bytes 147488 | tf_op jit(solution)/shard_map/ppermute | solution.py:289
  298.8 6.7 %collective-permute-start.48 = (bf16[1,96,768]{2,1,0:T(8,128)(2,1)S(1)}, bf16[1,96,768]{2,1,0:T(8,128)(2,1)S(1)}, u32[]{:S(2)}, u32[]{:S(2)}) collective-permute-start(bf16[1,96,768]{2,1,0:T(8,128)(2,1)S(1)} %get-tuple-element.136), channel_id=1, source_target_pairs={{0,8},{1,9},{2,10},{3,11},{4,12},{5,13},{6,14},{7,15},{8,0},{9,1},... | collective-permute-start | bytes 442376 | tf_op jit(solution)/shard_map/ppermute | solution.py:289
  305.5 5.8 %collective-permute-done.43 = bf16[1,96,768]{2,1,0:T(8,128)(2,1)S(1)} collective-permute-done((bf16[1,96,768]{2,1,0:T(8,128)(2,1)S(1)}, bf16[1,96,768]{2,1,0:T(8,128)(2,1)S(1)}, u32[]{:S(2)}, u32[]{:S(2)}) %collective-permute-start.43) | collective-permute-done | bytes 147488 | tf_op jit(solution)/shard_map/ppermute | solution.py:289
  311.5 6.9 %collective-permute-start.57 = (bf16[48,768]{1,0:T(8,128)(2,1)S(1)}, bf16[48,768]{1,0:T(8,128)(2,1)S(1)}, u32[]{:S(2)}, u32[]{:S(2)}) collective-permute-start(bf16[48,768]{1,0:T(8,128)(2,1)S(1)} %select_bitcast_fusion.5), channel_id=1, source_target_pairs={{0,2},{1,3},{2,0},{3,1},{4,6},{5,7},{6,4},{7,5},{8,10},{9,11},{10,... | collective-permute-start | bytes 221192 | tf_op jit(solution)/shard_map/ppermute | solution.py:289
  318.5 5.5 %collective-permute-done.49 = bf16[1,96,768]{2,1,0:T(8,128)(2,1)S(1)} collective-permute-done((bf16[1,96,768]{2,1,0:T(8,128)(2,1)S(1)}, bf16[1,96,768]{2,1,0:T(8,128)(2,1)S(1)}, u32[]{:S(2)}, u32[]{:S(2)}) %collective-permute-start.49) | collective-permute-done | bytes 147488 | tf_op jit(solution)/shard_map/ppermute | solution.py:289
  324.1 1.3 collective-permute-start.51
  327.3 1.5 convert_add_fusion
  328.8 6.6 %collective-permute-done.34 = bf16[4,48,1664]{2,1,0:T(8,128)(2,1)S(1)} collective-permute-done((bf16[4,48,1664]{2,1,0:T(8,128)(2,1)S(1)}, bf16[4,48,1664]{2,1,0:T(8,128)(2,1)S(1)}, u32[]{:S(2)}, u32[]{:S(2)}) %collective-permute-start.34) | collective-permute-done | bytes 639008 | tf_op jit(solution)/shard_map/ppermute | solution.py:289
  335.7 1.3 collective-permute-start.37
  336.9 1.4 collective-permute-start.36
  338.3 2.0 collective-permute-done.35
  340.4 3.5 collective-permute-done.37
  343.9 8.0 %collective-permute-done.36 = bf16[1,48,1664]{2,1,0:T(8,128)(2,1)S(1)} collective-permute-done((bf16[1,48,1664]{2,1,0:T(8,128)(2,1)S(1)}, bf16[1,48,1664]{2,1,0:T(8,128)(2,1)S(1)}, u32[]{:S(2)}, u32[]{:S(2)}) %collective-permute-start.36) | collective-permute-done | bytes 159776 | tf_op jit(solution)/shard_map/ppermute | solution.py:289
  352.2 4.0 %collective-permute-done.38 = bf16[48,1664]{1,0:T(8,128)(2,1)S(1)} collective-permute-done((bf16[48,1664]{1,0:T(8,128)(2,1)S(1)}, bf16[48,1664]{1,0:T(8,128)(2,1)S(1)}, u32[]{:S(2)}, u32[]{:S(2)}) %collective-permute-start.38) | collective-permute-done | bytes 159776 | tf_op jit(solution)/shard_map/ppermute | solution.py:289
  356.3 2.9 collective-permute-start.39
  (265 shorter events, 51.8 us)
Async XLA Ops:
  1.3 5.5 %collective-permute-start = (f32[8,128]{1,0:T(8,128)S(1)}, f32[8,128]{1,0:T(8,128)S(1)}, u32[]{:S(2)}, u32[]{:S(2)}) collective-permute-start(f32[8,128]{1,0:T(8,128)S(1)} %broadcast_in_dim.11), channel_id=1, source_target_pairs={{0,2},{1,3},{2,0},{3,1},{4,6},{5,7},{6,4},{7,5},{8,10},{9,11},{10,... | collective-permute-start | bytes 12296 | tf_op jit(solution)/shard_map/ppermute | solution.py:289
  3.8 4.7 %collective-permute-start.2 = (bf16[48,1280]{1,0:T(8,128)(2,1)S(1)}, bf16[48,1280]{1,0:T(8,128)(2,1)S(1)}, u32[]{:S(2)}, u32[]{:S(2)}) collective-permute-start(bf16[48,1280]{1,0:T(8,128)(2,1)S(1)} %fusion.11), channel_id=1, source_target_pairs={{0,2},{1,3},{2,0},{3,1},{4,6},{5,7},{6,4},{7,5},{8,10},{9,11},{10,... | collective-permute-start | bytes 368648 | tf_op jit(solution)/shard_map/ppermute | solution.py:289
  4.7 9.6 %collective-permute-start.11 = (bf16[3,48,768]{2,1,0:T(8,128)(2,1)S(1)}, bf16[3,48,768]{2,1,0:T(8,128)(2,1)S(1)}, u32[]{:S(2)}, u32[]{:S(2)}) collective-permute-start(bf16[3,48,768]{2,1,0:T(8,128)(2,1)S(1)} %select_bitcast_fusion), channel_id=1, source_target_pairs={{0,2},{1,3},{2,0},{3,1},{4,6},{5,7},{6,4},{7,5},{8,10},{9,11},{10,... | collective-permute-start | bytes 663560 | tf_op jit(solution)/shard_map/ppermute | solution.py:289
  6.0 48.0 %copy-start.4 = (bf16[512,768]{0,1:T(8,128)(2,1)}, bf16[512,768]{0,1:T(8,128)(2,1)S(1)}, u32[]{:S(2)}) copy-start(bf16[512,768]{0,1:T(8,128)(2,1)S(1)} %copy.135) | copy-start | bytes 2359300
  8.7 9.8 %collective-permute-start.5 = (bf16[1,48,1664]{2,1,0:T(8,128)(2,1)S(1)}, bf16[1,48,1664]{2,1,0:T(8,128)(2,1)S(1)}, u32[]{:S(2)}, u32[]{:S(2)}) collective-permute-start(bf16[1,48,1664]{2,1,0:T(8,128)(2,1)S(1)} %maximum_bitcast_fusion), channel_id=1, source_target_pairs={{0,24},{1,25},{2,26},{3,27},{4,28},{5,29},{6,30},{7,31},{8,16},{9,... | collective-permute-start | bytes 479240 | tf_op jit(solution)/shard_map/ppermute | solution.py:289
  13.3 22.9 %collective-permute-start.4 = (bf16[1,48,1664]{2,1,0:T(8,128)(2,1)S(1)}, bf16[1,48,1664]{2,1,0:T(8,128)(2,1)S(1)}, u32[]{:S(2)}, u32[]{:S(2)}) collective-permute-start(bf16[1,48,1664]{2,1,0:T(8,128)(2,1)S(1)} %maximum_bitcast_fusion), channel_id=1, source_target_pairs={{0,16},{1,17},{2,18},{3,19},{4,20},{5,21},{6,22},{7,23},{8,24},{9,... | collective-permute-start | bytes 479240 | tf_op jit(solution)/shard_map/ppermute | solution.py:289
  13.3 22.9 %collective-permute-start.3 = (bf16[1,48,1664]{2,1,0:T(8,128)(2,1)S(1)}, bf16[1,48,1664]{2,1,0:T(8,128)(2,1)S(1)}, u32[]{:S(2)}, u32[]{:S(2)}) collective-permute-start(bf16[1,48,1664]{2,1,0:T(8,128)(2,1)S(1)} %maximum_bitcast_fusion), channel_id=1, source_target_pairs={{0,8},{1,9},{2,10},{3,11},{4,12},{5,13},{6,14},{7,15},{8,0},{9,1},... | collective-permute-start | bytes 479240 | tf_op jit(solution)/shard_map/ppermute | solution.py:289
  14.4 33.5 %collective-permute-start.14 = (bf16[1,96,768]{2,1,0:T(8,128)(2,1)S(1)}, bf16[1,96,768]{2,1,0:T(8,128)(2,1)S(1)}, u32[]{:S(2)}, u32[]{:S(2)}) collective-permute-start(bf16[1,96,768]{2,1,0:T(8,128)(2,1)S(1)} %bitcast.152), channel_id=1, source_target_pairs={{0,24},{1,25},{2,26},{3,27},{4,28},{5,29},{6,30},{7,31},{8,16},{9,... | collective-permute-start | bytes 442376 | tf_op jit(solution)/shard_map/ppermute | solution.py:289
  18.4 21.3 %collective-permute-start.24 = (bf16[1,96,768]{2,1,0:T(8,128)(2,1)S(1)}, bf16[1,96,768]{2,1,0:T(8,128)(2,1)S(1)}, u32[]{:S(2)}, u32[]{:S(2)}) collective-permute-start(bf16[1,96,768]{2,1,0:T(8,128)(2,1)S(1)} %bitcast.157), channel_id=1, source_target_pairs={{0,24},{1,25},{2,26},{3,27},{4,28},{5,29},{6,30},{7,31},{8,16},{9,... | collective-permute-start | bytes 442376 | tf_op jit(solution)/shard_map/ppermute | solution.py:289
  18.5 27.2 %collective-permute-start.23 = (bf16[1,96,768]{2,1,0:T(8,128)(2,1)S(1)}, bf16[1,96,768]{2,1,0:T(8,128)(2,1)S(1)}, u32[]{:S(2)}, u32[]{:S(2)}) collective-permute-start(bf16[1,96,768]{2,1,0:T(8,128)(2,1)S(1)} %bitcast.159), channel_id=1, source_target_pairs={{0,16},{1,17},{2,18},{3,19},{4,20},{5,21},{6,22},{7,23},{8,24},{9,... | collective-permute-start | bytes 442376 | tf_op jit(solution)/shard_map/ppermute | solution.py:289
  36.2 9.5 %collective-permute-start.22 = (bf16[1,96,768]{2,1,0:T(8,128)(2,1)S(1)}, bf16[1,96,768]{2,1,0:T(8,128)(2,1)S(1)}, u32[]{:S(2)}, u32[]{:S(2)}) collective-permute-start(bf16[1,96,768]{2,1,0:T(8,128)(2,1)S(1)} %bitcast.160), channel_id=1, source_target_pairs={{0,8},{1,9},{2,10},{3,11},{4,12},{5,13},{6,14},{7,15},{8,0},{9,1},... | collective-permute-start | bytes 442376 | tf_op jit(solution)/shard_map/ppermute | solution.py:289
  36.3 12.2 %collective-permute-start.6 = (bf16[4,48,1664]{2,1,0:T(8,128)(2,1)S(1)}, bf16[4,48,1664]{2,1,0:T(8,128)(2,1)S(1)}, u32[]{:S(2)}, u32[]{:S(2)}) collective-permute-start(bf16[4,48,1664]{2,1,0:T(8,128)(2,1)S(1)} %pad_maximum_fusion), channel_id=1, source_target_pairs={{0,4},{1,5},{2,3},{3,2},{4,0},{5,1},{6,7},{7,6},{8,12},{9,13},{10,... | collective-permute-start | bytes 1916936 | tf_op jit(solution)/shard_map/ppermute | solution.py:289
  39.6 14.4 %collective-permute-start.13 = (bf16[1,96,768]{2,1,0:T(8,128)(2,1)S(1)}, bf16[1,96,768]{2,1,0:T(8,128)(2,1)S(1)}, u32[]{:S(2)}, u32[]{:S(2)}) collective-permute-start(bf16[1,96,768]{2,1,0:T(8,128)(2,1)S(1)} %bitcast.154), channel_id=1, source_target_pairs={{0,16},{1,17},{2,18},{3,19},{4,20},{5,21},{6,22},{7,23},{8,24},{9,... | collective-permute-start | bytes 442376 | tf_op jit(solution)/shard_map/ppermute | solution.py:289
  45.7 11.6 %collective-permute-start.12 = (bf16[1,96,768]{2,1,0:T(8,128)(2,1)S(1)}, bf16[1,96,768]{2,1,0:T(8,128)(2,1)S(1)}, u32[]{:S(2)}, u32[]{:S(2)}) collective-permute-start(bf16[1,96,768]{2,1,0:T(8,128)(2,1)S(1)} %bitcast.155), channel_id=1, source_target_pairs={{0,8},{1,9},{2,10},{3,11},{4,12},{5,13},{6,14},{7,15},{8,0},{9,1},... | collective-permute-start | bytes 442376 | tf_op jit(solution)/shard_map/ppermute | solution.py:289
  45.7 13.7 %collective-permute-start.19 = (bf16[1,96,768]{2,1,0:T(8,128)(2,1)S(1)}, bf16[1,96,768]{2,1,0:T(8,128)(2,1)S(1)}, u32[]{:S(2)}, u32[]{:S(2)}) collective-permute-start(bf16[1,96,768]{2,1,0:T(8,128)(2,1)S(1)} %bitcast.148), channel_id=1, source_target_pairs={{0,24},{1,25},{2,26},{3,27},{4,28},{5,29},{6,30},{7,31},{8,16},{9,... | collective-permute-start | bytes 442376 | tf_op jit(solution)/shard_map/ppermute | solution.py:289
  48.0 16.7 %collective-permute-start.18 = (bf16[1,96,768]{2,1,0:T(8,128)(2,1)S(1)}, bf16[1,96,768]{2,1,0:T(8,128)(2,1)S(1)}, u32[]{:S(2)}, u32[]{:S(2)}) collective-permute-start(bf16[1,96,768]{2,1,0:T(8,128)(2,1)S(1)} %bitcast.149), channel_id=1, source_target_pairs={{0,16},{1,17},{2,18},{3,19},{4,20},{5,21},{6,22},{7,23},{8,24},{9,... | collective-permute-start | bytes 442376 | tf_op jit(solution)/shard_map/ppermute | solution.py:289
  48.5 17.4 %collective-permute-start.17 = (bf16[1,96,768]{2,1,0:T(8,128)(2,1)S(1)}, bf16[1,96,768]{2,1,0:T(8,128)(2,1)S(1)}, u32[]{:S(2)}, u32[]{:S(2)}) collective-permute-start(bf16[1,96,768]{2,1,0:T(8,128)(2,1)S(1)} %bitcast.150), channel_id=1, source_target_pairs={{0,8},{1,9},{2,10},{3,11},{4,12},{5,13},{6,14},{7,15},{8,0},{9,1},... | collective-permute-start | bytes 442376 | tf_op jit(solution)/shard_map/ppermute | solution.py:289
  54.0 17.1 %collective-permute-start.1 = (bf16[512,768]{0,1:T(8,128)(2,1)S(1)}, bf16[512,768]{0,1:T(8,128)(2,1)S(1)}, u32[]{:S(2)}, u32[]{:S(2)}) collective-permute-start(bf16[512,768]{0,1:T(8,128)(2,1)S(1)} %copy.135), channel_id=1, source_target_pairs={{0,2},{1,3},{2,0},{3,1},{4,6},{5,7},{6,4},{7,5},{8,10},{9,11},{10,... | collective-permute-start | bytes 2359304 | tf_op jit(solution)/shard_map/ppermute | solution.py:289
  57.3 39.7 %collective-permute-start.7 = (bf16[8,48,1664]{2,1,0:T(8,128)(2,1)}, bf16[8,48,1664]{2,1,0:T(8,128)(2,1)}, u32[]{:S(2)}, u32[]{:S(2)}) collective-permute-start(bf16[8,48,1664]{2,1,0:T(8,128)(2,1)} %constant_dynamic-update-slice_fusion.first), channel_id=1, source_target_pairs={{0,1},{1,0},{2,6},{3,7},{4,5},{5,4},{6,2},{7,3},{8,9},{9,8},{10,14... | collective-permute-start | bytes 3833864 | tf_op jit(solution)/shard_map/ppermute | solution.py:289
  59.4 60.5 %collective-permute-start.15 = (bf16[4,96,768]{2,1,0:T(8,128)(2,1)}, bf16[4,96,768]{2,1,0:T(8,128)(2,1)}, u32[]{:S(2)}, u32[]{:S(2)}) collective-permute-start(bf16[4,96,768]{2,1,0:T(8,128)(2,1)} %pad_maximum_fusion.1), channel_id=1, source_target_pairs={{0,4},{1,5},{2,3},{3,2},{4,0},{5,1},{6,7},{7,6},{8,12},{9,13},{10,... | collective-permute-start | bytes 1769480 | tf_op jit(solution)/shard_map/ppermute | solution.py:289
  64.7 65.8 %collective-permute-start.25 = (bf16[4,96,768]{2,1,0:T(8,128)(2,1)S(1)}, bf16[4,96,768]{2,1,0:T(8,128)(2,1)S(1)}, u32[]{:S(2)}, u32[]{:S(2)}) collective-permute-start(bf16[4,96,768]{2,1,0:T(8,128)(2,1)S(1)} %pad_maximum_fusion.3), channel_id=1, source_target_pairs={{0,4},{1,5},{2,3},{3,2},{4,0},{5,1},{6,7},{7,6},{8,12},{9,13},{10,... | collective-permute-start | bytes 1769480 | tf_op jit(solution)/shard_map/ppermute | solution.py:289
  66.8 28.0 %collective-permute-start.20 = (bf16[4,96,768]{2,1,0:T(8,128)(2,1)}, bf16[4,96,768]{2,1,0:T(8,128)(2,1)}, u32[]{:S(2)}, u32[]{:S(2)}) collective-permute-start(bf16[4,96,768]{2,1,0:T(8,128)(2,1)} %pad_maximum_fusion.2), channel_id=1, source_target_pairs={{0,4},{1,5},{2,3},{3,2},{4,0},{5,1},{6,7},{7,6},{8,12},{9,13},{10,... | collective-permute-start | bytes 1769480 | tf_op jit(solution)/shard_map/ppermute | solution.py:289
  71.1 25.6 %copy-start.5 = (bf16[512,768]{0,1:T(8,128)(2,1)}, bf16[512,768]{0,1:T(8,128)(2,1)S(1)}, u32[]{:S(2)}) copy-start(bf16[512,768]{0,1:T(8,128)(2,1)S(1)} %collective-permute-done.1) | copy-start | bytes 2359300
  96.7 39.7 %collective-permute-start.21 = (bf16[8,96,768]{2,1,0:T(8,128)(2,1)}, bf16[8,96,768]{2,1,0:T(8,128)(2,1)}, u32[]{:S(2)}, u32[]{:S(2)}) collective-permute-start(bf16[8,96,768]{2,1,0:T(8,128)(2,1)} %constant_dynamic-update-slice_fusion.10.value_a), channel_id=1, source_target_pairs={{0,1},{1,0},{2,6},{3,7},{4,5},{5,4},{6,2},{7,3},{8,9},{9,8},{10,14... | collective-permute-start | bytes 3538952 | tf_op jit(solution)/shard_map/ppermute | solution.py:289
  104.0 19.2 %collective-permute-start.9 = (bf16[8,48,768]{2,1,0:T(8,128)(2,1)}, bf16[8,48,768]{2,1,0:T(8,128)(2,1)S(1)}, u32[]{:S(2)}, u32[]{:S(2)}) collective-permute-start(bf16[8,48,768]{2,1,0:T(8,128)(2,1)} %get-tuple-element.47.w_mine), channel_id=1, source_target_pairs={{0,2},{1,3},{2,0},{3,1},{4,6},{5,7},{6,4},{7,5},{8,10},{9,11},{10,... | collective-permute-start | bytes 1769480 | tf_op jit(solution)/shard_map/ppermute | solution.py:289
  119.4 3.9 %collective-permute-start.8 = (bf16[512,384]{1,0:T(8,128)(2,1)S(1)}, bf16[512,384]{1,0:T(8,128)(2,1)S(1)}, u32[]{:S(2)}, u32[]{:S(2)}) collective-permute-start(bf16[512,384]{1,0:T(8,128)(2,1)S(1)} %get-tuple-element.126), channel_id=1, source_target_pairs={{0,2},{1,3},{2,0},{3,1},{4,6},{5,7},{6,4},{7,5},{8,10},{9,11},{10,... | collective-permute-start | bytes 1179656 | tf_op jit(solution)/shard_map/ppermute | solution.py:289
  121.8 15.7 %collective-permute-start.16 = (bf16[8,96,768]{2,1,0:T(8,128)(2,1)}, bf16[8,96,768]{2,1,0:T(8,128)(2,1)}, u32[]{:S(2)}, u32[]{:S(2)}) collective-permute-start(bf16[8,96,768]{2,1,0:T(8,128)(2,1)} %constant_dynamic-update-slice_fusion.5.gate_a), channel_id=1, source_target_pairs={{0,1},{1,0},{2,6},{3,7},{4,5},{5,4},{6,2},{7,3},{8,9},{9,8},{10,14... | collective-permute-start | bytes 3538952 | tf_op jit(solution)/shard_map/ppermute | solution.py:289
  130.2 5.0 %collective-permute-start.10 = (bf16[512,768]{0,1:T(8,128)(2,1)S(1)}, bf16[512,768]{0,1:T(8,128)(2,1)S(1)}, u32[]{:S(2)}, u32[]{:S(2)}) collective-permute-start(bf16[512,768]{0,1:T(8,128)(2,1)S(1)} %copy.141), channel_id=1, source_target_pairs={{0,2},{1,3},{2,0},{3,1},{4,6},{5,7},{6,4},{7,5},{8,10},{9,11},{10,... | collective-permute-start | bytes 2359304 | tf_op jit(solution)/shard_map/ppermute | solution.py:289
  131.3 19.6 %collective-permute-start.26 = (bf16[8,96,768]{2,1,0:T(8,128)(2,1)}, bf16[8,96,768]{2,1,0:T(8,128)(2,1)S(1)}, u32[]{:S(2)}, u32[]{:S(2)}) collective-permute-start(bf16[8,96,768]{2,1,0:T(8,128)(2,1)} %constant_dynamic-update-slice_fusion.15.down_a), channel_id=1, source_target_pairs={{0,1},{1,0},{2,6},{3,7},{4,5},{5,4},{6,2},{7,3},{8,9},{9,8},{10,14... | collective-permute-start | bytes 3538952 | tf_op jit(solution)/shard_map/ppermute | solution.py:289
  159.9 3.1 collective-permute-start.27
  169.6 22.2 %copy-start.16 = (bf16[512,768]{0,1:T(8,128)(2,1)}, bf16[512,768]{0,1:T(8,128)(2,1)S(1)}, u32[]{:S(2)}) copy-start(bf16[512,768]{0,1:T(8,128)(2,1)S(1)} %copy.147) | copy-start | bytes 2359300
  169.6 2.4 collective-permute-start.28
  172.0 19.9 %copy-start.17 = (bf16[512,768]{0,1:T(8,128)(2,1)}, bf16[512,768]{0,1:T(8,128)(2,1)S(1)}, u32[]{:S(2)}) copy-start(bf16[512,768]{0,1:T(8,128)(2,1)S(1)} %collective-permute-done.28) | copy-start | bytes 2359300
  173.1 19.2 %copy-start.24 = (f32[8,768]{1,0:T(8,128)S(1)}, f32[8,768]{1,0:T(8,128)}, u32[]{:S(2)}) copy-start(f32[8,768]{1,0:T(8,128)} %get-tuple-element.78) | copy-start | bytes 73732
  191.9 33.6 %collective-permute-start.29 = (bf16[512,768]{1,0:T(8,128)(2,1)}, bf16[512,768]{1,0:T(8,128)(2,1)S(1)}, u32[]{:S(2)}, u32[]{:S(2)}) collective-permute-start(bf16[512,768]{1,0:T(8,128)(2,1)} %get-tuple-element.64), channel_id=1, source_target_pairs={{0,2},{1,3},{2,0},{3,1},{4,6},{5,7},{6,4},{7,5},{8,10},{9,11},{10,... | collective-permute-start | bytes 2359304 | tf_op jit(solution)/shard_map/ppermute | solution.py:289
  202.2 59.7 %collective-permute-start.52 = (bf16[8,96,768]{2,1,0:T(8,128)(2,1)}, bf16[8,96,768]{2,1,0:T(8,128)(2,1)S(1)}, u32[]{:S(2)}, u32[]{:S(2)}) collective-permute-start(bf16[8,96,768]{2,1,0:T(8,128)(2,1)} %slice.391), channel_id=1, source_target_pairs={{0,1},{1,0},{2,6},{3,7},{4,5},{5,4},{6,2},{7,3},{8,9},{9,8},{10,14... | collective-permute-start | bytes 3538952 | tf_op jit(solution)/shard_map/ppermute | solution.py:289
  224.0 39.1 %collective-permute-start.40 = (bf16[8,96,768]{2,1,0:T(8,128)(2,1)}, bf16[8,96,768]{2,1,0:T(8,128)(2,1)}, u32[]{:S(2)}, u32[]{:S(2)}) collective-permute-start(bf16[8,96,768]{2,1,0:T(8,128)(2,1)} %slice.371), channel_id=1, source_target_pairs={{0,1},{1,0},{2,6},{3,7},{4,5},{5,4},{6,2},{7,3},{8,9},{9,8},{10,14... | collective-permute-start | bytes 3538952 | tf_op jit(solution)/shard_map/ppermute | solution.py:289
  224.0 42.5 %collective-permute-start.46 = (bf16[8,96,768]{2,1,0:T(8,128)(2,1)}, bf16[8,96,768]{2,1,0:T(8,128)(2,1)S(1)}, u32[]{:S(2)}, u32[]{:S(2)}) collective-permute-start(bf16[8,96,768]{2,1,0:T(8,128)(2,1)} %slice.381), channel_id=1, source_target_pairs={{0,1},{1,0},{2,6},{3,7},{4,5},{5,4},{6,2},{7,3},{8,9},{9,8},{10,14... | collective-permute-start | bytes 3538952 | tf_op jit(solution)/shard_map/ppermute | solution.py:289
  234.0 4.3 %collective-permute-start.30 = (bf16[512,384]{1,0:T(8,128)(2,1)}, bf16[512,384]{1,0:T(8,128)(2,1)S(1)}, u32[]{:S(2)}, u32[]{:S(2)}) collective-permute-start(bf16[512,384]{1,0:T(8,128)(2,1)} %get-tuple-element.68), channel_id=1, source_target_pairs={{0,2},{1,3},{2,0},{3,1},{4,6},{5,7},{6,4},{7,5},{8,10},{9,11},{10,... | collective-permute-start | bytes 1179656 | tf_op jit(solution)/shard_map/ppermute | solution.py:289
  237.5 30.1 %collective-permute-start.32 = (bf16[8,48,768]{2,1,0:T(8,128)(2,1)}, bf16[8,48,768]{2,1,0:T(8,128)(2,1)}, u32[]{:S(2)}, u32[]{:S(2)}) collective-permute-start(bf16[8,48,768]{2,1,0:T(8,128)(2,1)} %fusion.1), channel_id=1, source_target_pairs={{0,2},{1,3},{2,0},{3,1},{4,6},{5,7},{6,4},{7,5},{8,10},{9,11},{10,... | collective-permute-start | bytes 1769480 | tf_op jit(solution)/shard_map/ppermute | solution.py:289
  261.4 65.1 %collective-permute-start.31 = (bf16[512,768]{1,0:T(8,128)(2,1)}, bf16[512,768]{1,0:T(8,128)(2,1)S(1)}, u32[]{:S(2)}, u32[]{:S(2)}) collective-permute-start(bf16[512,768]{1,0:T(8,128)(2,1)} %get-tuple-element.75), channel_id=1, source_target_pairs={{0,2},{1,3},{2,0},{3,1},{4,6},{5,7},{6,4},{7,5},{8,10},{9,11},{10,... | collective-permute-start | bytes 2359304 | tf_op jit(solution)/shard_map/ppermute | solution.py:289
  263.1 19.6 %collective-permute-start.53 = (bf16[4,96,768]{2,1,0:T(8,128)(2,1)}, bf16[4,96,768]{2,1,0:T(8,128)(2,1)S(1)}, u32[]{:S(2)}, u32[]{:S(2)}) collective-permute-start(bf16[4,96,768]{2,1,0:T(8,128)(2,1)} %slice.393), channel_id=1, source_target_pairs={{0,4},{1,5},{2,3},{3,2},{4,0},{5,1},{6,7},{7,6},{8,12},{9,13},{10,... | collective-permute-start | bytes 1769480 | tf_op jit(solution)/shard_map/ppermute | solution.py:289
  265.7 17.3 %collective-permute-start.41 = (bf16[4,96,768]{2,1,0:T(8,128)(2,1)S(1)}, bf16[4,96,768]{2,1,0:T(8,128)(2,1)S(1)}, u32[]{:S(2)}, u32[]{:S(2)}) collective-permute-start(bf16[4,96,768]{2,1,0:T(8,128)(2,1)S(1)} %slice.373), channel_id=1, source_target_pairs={{0,4},{1,5},{2,3},{3,2},{4,0},{5,1},{6,7},{7,6},{8,12},{9,13},{10,... | collective-permute-start | bytes 1769480 | tf_op jit(solution)/shard_map/ppermute | solution.py:289
  266.9 18.5 %collective-permute-start.47 = (bf16[4,96,768]{2,1,0:T(8,128)(2,1)S(1)}, bf16[4,96,768]{2,1,0:T(8,128)(2,1)S(1)}, u32[]{:S(2)}, u32[]{:S(2)}) collective-permute-start(bf16[4,96,768]{2,1,0:T(8,128)(2,1)S(1)} %slice.383), channel_id=1, source_target_pairs={{0,4},{1,5},{2,3},{3,2},{4,0},{5,1},{6,7},{7,6},{8,12},{9,13},{10,... | collective-permute-start | bytes 1769480 | tf_op jit(solution)/shard_map/ppermute | solution.py:289
  278.5 46.9 %collective-permute-start.33 = (bf16[8,48,1664]{2,1,0:T(8,128)(2,1)S(1)}, bf16[8,48,1664]{2,1,0:T(8,128)(2,1)S(1)}, u32[]{:S(2)}, u32[]{:S(2)}) collective-permute-start(bf16[8,48,1664]{2,1,0:T(8,128)(2,1)S(1)} %slice.355), channel_id=1, source_target_pairs={{0,1},{1,0},{2,6},{3,7},{4,5},{5,4},{6,2},{7,3},{8,9},{9,8},{10,14... | collective-permute-start | bytes 3833864 | tf_op jit(solution)/shard_map/ppermute | solution.py:289
  282.9 4.8 %collective-permute-start.54 = (bf16[1,96,768]{2,1,0:T(8,128)(2,1)S(1)}, bf16[1,96,768]{2,1,0:T(8,128)(2,1)S(1)}, u32[]{:S(2)}, u32[]{:S(2)}) collective-permute-start(bf16[1,96,768]{2,1,0:T(8,128)(2,1)S(1)} %get-tuple-element.133), channel_id=1, source_target_pairs={{0,8},{1,9},{2,10},{3,11},{4,12},{5,13},{6,14},{7,15},{8,0},{9,1},... | collective-permute-start | bytes 442376 | tf_op jit(solution)/shard_map/ppermute | solution.py:289
  283.0 7.6 %collective-permute-start.56 = (bf16[1,96,768]{2,1,0:T(8,128)(2,1)S(1)}, bf16[1,96,768]{2,1,0:T(8,128)(2,1)S(1)}, u32[]{:S(2)}, u32[]{:S(2)}) collective-permute-start(bf16[1,96,768]{2,1,0:T(8,128)(2,1)S(1)} %get-tuple-element.134), channel_id=1, source_target_pairs={{0,24},{1,25},{2,26},{3,27},{4,28},{5,29},{6,30},{7,31},{8,16},{9,... | collective-permute-start | bytes 442376 | tf_op jit(solution)/shard_map/ppermute | solution.py:289
  285.4 13.3 %collective-permute-start.55 = (bf16[1,96,768]{2,1,0:T(8,128)(2,1)S(1)}, bf16[1,96,768]{2,1,0:T(8,128)(2,1)S(1)}, u32[]{:S(2)}, u32[]{:S(2)}) collective-permute-start(bf16[1,96,768]{2,1,0:T(8,128)(2,1)S(1)} %get-tuple-element.135), channel_id=1, source_target_pairs={{0,16},{1,17},{2,18},{3,19},{4,20},{5,21},{6,22},{7,23},{8,24},{9,... | collective-permute-start | bytes 442376 | tf_op jit(solution)/shard_map/ppermute | solution.py:289
  287.6 11.1 %collective-permute-start.42 = (bf16[1,96,768]{2,1,0:T(8,128)(2,1)S(1)}, bf16[1,96,768]{2,1,0:T(8,128)(2,1)S(1)}, u32[]{:S(2)}, u32[]{:S(2)}) collective-permute-start(bf16[1,96,768]{2,1,0:T(8,128)(2,1)S(1)} %get-tuple-element.139), channel_id=1, source_target_pairs={{0,8},{1,9},{2,10},{3,11},{4,12},{5,13},{6,14},{7,15},{8,0},{9,1},... | collective-permute-start | bytes 442376 | tf_op jit(solution)/shard_map/ppermute | solution.py:289
  290.6 14.9 %collective-permute-start.44 = (bf16[1,96,768]{2,1,0:T(8,128)(2,1)S(1)}, bf16[1,96,768]{2,1,0:T(8,128)(2,1)S(1)}, u32[]{:S(2)}, u32[]{:S(2)}) collective-permute-start(bf16[1,96,768]{2,1,0:T(8,128)(2,1)S(1)} %get-tuple-element.140), channel_id=1, source_target_pairs={{0,24},{1,25},{2,26},{3,27},{4,28},{5,29},{6,30},{7,31},{8,16},{9,... | collective-permute-start | bytes 442376 | tf_op jit(solution)/shard_map/ppermute | solution.py:289
  298.7 12.7 %collective-permute-start.43 = (bf16[1,96,768]{2,1,0:T(8,128)(2,1)S(1)}, bf16[1,96,768]{2,1,0:T(8,128)(2,1)S(1)}, u32[]{:S(2)}, u32[]{:S(2)}) collective-permute-start(bf16[1,96,768]{2,1,0:T(8,128)(2,1)S(1)} %get-tuple-element.141), channel_id=1, source_target_pairs={{0,16},{1,17},{2,18},{3,19},{4,20},{5,21},{6,22},{7,23},{8,24},{9,... | collective-permute-start | bytes 442376 | tf_op jit(solution)/shard_map/ppermute | solution.py:289
  298.7 26.7 %copy-start.2 = (bf16[16,48,1664]{2,1,0:T(8,128)(2,1)S(1)}, bf16[16,48,1664]{2,1,0:T(8,128)(2,1)}, u32[]{:S(2)}) copy-start(bf16[16,48,1664]{2,1,0:T(8,128)(2,1)} %qkv_grad.1) | copy-start | bytes 7667716
  298.8 12.7 %collective-permute-start.48 = (bf16[1,96,768]{2,1,0:T(8,128)(2,1)S(1)}, bf16[1,96,768]{2,1,0:T(8,128)(2,1)S(1)}, u32[]{:S(2)}, u32[]{:S(2)}) collective-permute-start(bf16[1,96,768]{2,1,0:T(8,128)(2,1)S(1)} %get-tuple-element.136), channel_id=1, source_target_pairs={{0,8},{1,9},{2,10},{3,11},{4,12},{5,13},{6,14},{7,15},{8,0},{9,1},... | collective-permute-start | bytes 442376 | tf_op jit(solution)/shard_map/ppermute | solution.py:289
  305.5 12.9 %collective-permute-start.50 = (bf16[1,96,768]{2,1,0:T(8,128)(2,1)S(1)}, bf16[1,96,768]{2,1,0:T(8,128)(2,1)S(1)}, u32[]{:S(2)}, u32[]{:S(2)}) collective-permute-start(bf16[1,96,768]{2,1,0:T(8,128)(2,1)S(1)} %get-tuple-element.137), channel_id=1, source_target_pairs={{0,24},{1,25},{2,26},{3,27},{4,28},{5,29},{6,30},{7,31},{8,16},{9,... | collective-permute-start | bytes 442376 | tf_op jit(solution)/shard_map/ppermute | solution.py:289
  311.3 12.6 %collective-permute-start.49 = (bf16[1,96,768]{2,1,0:T(8,128)(2,1)S(1)}, bf16[1,96,768]{2,1,0:T(8,128)(2,1)S(1)}, u32[]{:S(2)}, u32[]{:S(2)}) collective-permute-start(bf16[1,96,768]{2,1,0:T(8,128)(2,1)S(1)} %get-tuple-element.138), channel_id=1, source_target_pairs={{0,16},{1,17},{2,18},{3,19},{4,20},{5,21},{6,22},{7,23},{8,24},{9,... | collective-permute-start | bytes 442376 | tf_op jit(solution)/shard_map/ppermute | solution.py:289
  311.5 17.3 %collective-permute-start.57 = (bf16[48,768]{1,0:T(8,128)(2,1)S(1)}, bf16[48,768]{1,0:T(8,128)(2,1)S(1)}, u32[]{:S(2)}, u32[]{:S(2)}) collective-permute-start(bf16[48,768]{1,0:T(8,128)(2,1)S(1)} %select_bitcast_fusion.5), channel_id=1, source_target_pairs={{0,2},{1,3},{2,0},{3,1},{4,6},{5,7},{6,4},{7,5},{8,10},{9,11},{10,... | collective-permute-start | bytes 221192 | tf_op jit(solution)/shard_map/ppermute | solution.py:289
  318.4 10.4 %collective-permute-start.45 = (bf16[48,768]{1,0:T(8,128)(2,1)S(1)}, bf16[48,768]{1,0:T(8,128)(2,1)S(1)}, u32[]{:S(2)}, u32[]{:S(2)}) collective-permute-start(bf16[48,768]{1,0:T(8,128)(2,1)S(1)} %select_bitcast_fusion.7), channel_id=1, source_target_pairs={{0,2},{1,3},{2,0},{3,1},{4,6},{5,7},{6,4},{7,5},{8,10},{9,11},{10,... | collective-permute-start | bytes 221192 | tf_op jit(solution)/shard_map/ppermute | solution.py:289
  324.1 14.2 %collective-permute-start.51 = (bf16[48,768]{1,0:T(8,128)(2,1)S(1)}, bf16[48,768]{1,0:T(8,128)(2,1)S(1)}, u32[]{:S(2)}, u32[]{:S(2)}) collective-permute-start(bf16[48,768]{1,0:T(8,128)(2,1)S(1)} %select_bitcast_fusion.6), channel_id=1, source_target_pairs={{0,2},{1,3},{2,0},{3,1},{4,6},{5,7},{6,4},{7,5},{8,10},{9,11},{10,... | collective-permute-start | bytes 221192 | tf_op jit(solution)/shard_map/ppermute | solution.py:289
  325.8 9.6 %collective-permute-start.34 = (bf16[4,48,1664]{2,1,0:T(8,128)(2,1)S(1)}, bf16[4,48,1664]{2,1,0:T(8,128)(2,1)S(1)}, u32[]{:S(2)}, u32[]{:S(2)}) collective-permute-start(bf16[4,48,1664]{2,1,0:T(8,128)(2,1)S(1)} %slice.357), channel_id=1, source_target_pairs={{0,4},{1,5},{2,3},{3,2},{4,0},{5,1},{6,7},{7,6},{8,12},{9,13},{10,... | collective-permute-start | bytes 1916936 | tf_op jit(solution)/shard_map/ppermute | solution.py:289
  335.6 4.8 %collective-permute-start.35 = (bf16[1,48,1664]{2,1,0:T(8,128)(2,1)S(1)}, bf16[1,48,1664]{2,1,0:T(8,128)(2,1)S(1)}, u32[]{:S(2)}, u32[]{:S(2)}) collective-permute-start(bf16[1,48,1664]{2,1,0:T(8,128)(2,1)S(1)} %get-tuple-element.130), channel_id=1, source_target_pairs={{0,8},{1,9},{2,10},{3,11},{4,12},{5,13},{6,14},{7,15},{8,0},{9,1},... | collective-permute-start | bytes 479240 | tf_op jit(solution)/shard_map/ppermute | solution.py:289
  335.7 8.2 %collective-permute-start.37 = (bf16[1,48,1664]{2,1,0:T(8,128)(2,1)S(1)}, bf16[1,48,1664]{2,1,0:T(8,128)(2,1)S(1)}, u32[]{:S(2)}, u32[]{:S(2)}) collective-permute-start(bf16[1,48,1664]{2,1,0:T(8,128)(2,1)S(1)} %get-tuple-element.131), channel_id=1, source_target_pairs={{0,24},{1,25},{2,26},{3,27},{4,28},{5,29},{6,30},{7,31},{8,16},{9,... | collective-permute-start | bytes 479240 | tf_op jit(solution)/shard_map/ppermute | solution.py:289
  336.9 15.0 %collective-permute-start.36 = (bf16[1,48,1664]{2,1,0:T(8,128)(2,1)S(1)}, bf16[1,48,1664]{2,1,0:T(8,128)(2,1)S(1)}, u32[]{:S(2)}, u32[]{:S(2)}) collective-permute-start(bf16[1,48,1664]{2,1,0:T(8,128)(2,1)S(1)} %get-tuple-element.132), channel_id=1, source_target_pairs={{0,16},{1,17},{2,18},{3,19},{4,20},{5,21},{6,22},{7,23},{8,24},{9,... | collective-permute-start | bytes 479240 | tf_op jit(solution)/shard_map/ppermute | solution.py:289
  352.0 4.2 %collective-permute-start.38 = (bf16[48,1664]{1,0:T(8,128)(2,1)S(1)}, bf16[48,1664]{1,0:T(8,128)(2,1)S(1)}, u32[]{:S(2)}, u32[]{:S(2)}) collective-permute-start(bf16[48,1664]{1,0:T(8,128)(2,1)S(1)} %fusion.6), channel_id=1, source_target_pairs={{0,1},{1,0},{2,3},{3,2},{4,5},{5,4},{6,7},{7,6},{8,9},{9,8},{10,11... | collective-permute-start | bytes 479240 | tf_op jit(solution)/shard_map/ppermute | solution.py:289
  356.3 5.9 %collective-permute-start.39 = (bf16[48,1280]{1,0:T(8,128)(2,1)S(1)}, bf16[48,1280]{1,0:T(8,128)(2,1)S(1)}, u32[]{:S(2)}, u32[]{:S(2)}) collective-permute-start(bf16[48,1280]{1,0:T(8,128)(2,1)S(1)} %get-tuple-element.152), channel_id=1, source_target_pairs={{0,2},{1,3},{2,0},{3,1},{4,6},{5,7},{6,4},{7,5},{8,10},{9,11},{10,... | collective-permute-start | bytes 368648 | tf_op jit(solution)/shard_map/ppermute | solution.py:289
  (32 other events, 72.8 us)
